TPU v7x, 512 devices: a whole 4x4x16 slice. The times are simulated.
512 devices in a mesh: dp: 32 (over z, core), tensor: 16 (over x, y).
Axes of the slice: x: 4, y: 4, z: 16, core: 2. Of those that a mesh axis runs over, the one named last changes fastest.
Arguments:
- activations: bfloat16 [32768, 1024], P('dp'), may hold values from -6 to 6
- out_grads: bfloat16 [32768, 4096], P('dp', 'tensor'), may hold values from -0.1875 to 0.1875
- q_previous: float32 [64, 4096], P(None, 'tensor'), may hold values from -0.09375 to 0.09375
- carried_error: float32 [32, 1024, 4096], P('dp', None, 'tensor'), may hold values from -12 to 12
Outputs:
- q_factor: float32 [64, 4096], P(None, 'tensor')
- new_residual: float32 [32, 1024, 4096], P('dp', None, 'tensor')
All inputs are finite; a program needn't handle non-finite values.
Results may differ from a plain program's by a relative error of at most 0.0003.
Values sent between devices are 32-bit elements; how exact they have to be, the bound alone decides.
A program may use at most 64 MiB of HBM per device.

v0:
```python
import jax
import jax.numpy as jnp
from jax import lax
from jax.sharding import PartitionSpec as P

ridge_scale = 0.001
highest = lax.Precision.HIGHEST


def self_gram(p_rows):
    return lax.dot_general(
        p_rows,
        p_rows,
        (((0,), (0,)), ((), ())),
        precision=highest,
        preferred_element_type=jnp.float32,
    )


def orthonormal(p_rows, gram_matrix, total_rows):
    rank_size = gram_matrix.shape[0]
    ridge_shift = (
        ridge_scale * total_rows * (jnp.trace(gram_matrix) / (total_rows * rank_size) + 1e-05)
    )
    factor = jnp.linalg.cholesky(gram_matrix + ridge_shift * jnp.eye(rank_size, dtype=jnp.float32))
    return jax.scipy.linalg.solve_triangular(factor, p_rows.T, lower=True).T


def right_terms(spanning, columns):
    return lax.dot_general(
        spanning,
        columns,
        (((0,), (0,)), ((), ())),
        precision=highest,
        preferred_element_type=jnp.float32,
    )


def on_device(activations, out_grads, q_previous, carried_error):
    gradient = lax.dot_general(
        activations, out_grads, (((0,), (0,)), ((), ())), preferred_element_type=jnp.float32
    )
    merged = gradient + carried_error[0]
    partial_value = lax.dot_general(
        merged,
        q_previous,
        (((1,), (1,)), ((), ())),
        precision=highest,
        preferred_element_type=jnp.float32,
    )
    total_rows = merged.shape[0]
    p_sum = lax.psum(partial_value, ("dp", "tensor"))
    spanning = orthonormal(p_sum, self_gram(p_sum), total_rows)
    replica_count = lax.axis_size("dp")
    q_factor = lax.psum(right_terms(spanning, merged), "dp") / replica_count
    low_rank = jnp.dot(spanning, q_factor, precision=highest, preferred_element_type=jnp.float32)
    residual = merged - low_rank
    return (q_factor, residual[None])


def solution(mesh):
    placed = (P("dp", None), P("dp", "tensor"), P(None, "tensor"), P("dp", None, "tensor"))
    return jax.shard_map(
        on_device,
        mesh=mesh,
        in_specs=placed,
        out_specs=(P(None, "tensor"), P("dp", None, "tensor")),
        check_vma=False,
    )
```

profile of v0, /device:TPU:1, one launch (start us, length us, event | category | flops | bytes accessed | tf_op | source)
XLA Modules:
  0.0 682.8 jit_solution(14444543799267020030)
XLA Ops:
  7.2 0.0 copy-start
  7.2 0.0 copy-start.2
  7.2 0.0 all-reduce.3.cloned.1.call-start
  7.2 1.5 copy-done
  8.8 2.1 convolution_add_fusion
  10.9 0.0 copy-done.2
  10.9 1.8 fusion.6
  12.7 0.0 all-reduce.3.cloned.1.call-update
  12.8 0.0 all-reduce.5.cloned.1.call-start
  12.8 461.7 %all-reduce.3.cloned.1.call-done = f32[1024,64]{0,1:T(8,128)} async-done(((f32[1024,64]{0,1:T(8,128)}), f32[1024,64]{0,1:T(8,128)}) %all-reduce.3.cloned.1.call-update) | async-done | bytes 262160 | tf_op jit(solution)/shard_map/psum | solution.py:52
  474.5 2.0 select_reduce_fusion.1
  476.5 0.1 copy.6
  477.3 5.8 cholesky.17
  483.2 0.6 compare_reduce_fusion
  483.8 0.7 fusion.1
  484.5 4.9 custom-call.7
  489.4 1.4 fusion.2
  490.8 1.3 fusion.7
  492.0 0.0 all-reduce.5.cloned.1.call-update
  492.1 181.0 %all-reduce.5.cloned.1.call-done = f32[64,256]{1,0:T(8,128)} async-done(((f32[64,256]{1,0:T(8,128)}), f32[64,256]{1,0:T(8,128)}) %all-reduce.5.cloned.1.call-update) | async-done | bytes 65552 | tf_op jit(solution)/shard_map/psum | solution.py:55
  673.1 0.8 broadcast_multiply_fusion
  673.9 0.0 copy-start.1
  673.9 2.0 fusion
  675.9 0.0 copy-done.1
  (2 shorter events, 0.0 us)
Async XLA Ops:
  7.2 1.6 copy-start
  7.2 3.7 copy-start.2
  7.2 467.3 %all-reduce.3.cloned.1.call-start = ((), (), s32[]{:S(2)}) async-start(), calls=%async_computation | async-start | bytes 524288 | tf_op jit(solution)/shard_map/psum | solution.py:52
  12.8 660.3 %all-reduce.5.cloned.1.call-start = ((), (), s32[]{:S(2)}) async-start(), calls=%async_computation.1 | async-start | bytes 131072 | tf_op jit(solution)/shard_map/psum | solution.py:55
  673.9 2.0 copy-start.1
Sparse Core Ops, SparseCore 0:
  14.0 460.4 all-reduce.2
  492.2 180.8 all-reduce.4
where the time goes:
time: 683 us
  waiting for transfers between devices  643 us (94%)
  between operations  14.8 us (2%)
  other arithmetic  12.9 us (2%)
  matrix products  10.6 us (2%)
    psum x1, waiting for transfers between devices, on_device(): p_sum = lax.psum(partial_value, ('dp', 'tensor'))  462 us
    psum x1, waiting for transfers between devices, on_device(): q_factor = lax.psum(right_terms(spanning, merged), 'dp') / replica_count  181 us
  transfers between devices with their start and end apart: 2, of which 2 were waited for; matrix products, arithmetic and copies ran while one was open for 0% of the time, Pallas kernels for 0%

commit v1 on v0

v1 whole, which is shorter than its diff:
```python
import functools

import jax
import jax.numpy as jnp
from jax import lax
from jax.experimental import pallas as pl
from jax.experimental.pallas import tpu as pltpu
from jax.sharding import PartitionSpec as P

ridge_scale = 0.001
highest = lax.Precision.HIGHEST
f32 = jnp.float32
bf16 = jnp.bfloat16
MESH = pl.DeviceIdType.MESH
CORES = 2


def dot(a, b, ca, cb, precision=None):
    return lax.dot_general(
        a, b, (((ca,), (cb,)), ((), ())), precision=precision, preferred_element_type=f32
    )


def split(value):
    high = value.astype(bf16)
    return high, (value - high.astype(f32)).astype(bf16)


def dot3(a, b, ca, cb):
    return dot(a[0], b[0], ca, cb) + (dot(a[0], b[1], ca, cb) + dot(a[1], b[0], ca, cb))


def await_bytes(ref, sem):
    pltpu.make_async_copy(ref, ref, sem).wait()


def ring_order(n):
    return sorted(range(1, n), key=lambda k: -min(k, n - k))


def kernel(
    nx, ny, nz,
    act_hbm, grad_hbm, q_hbm, err_hbm, factor_ref, res_hbm,
    act, grads, q_prev, err, merged, part, from_core, half, xy_in, z_out, z_in, p_t,
    n_own, pair_in, cross_out, cross_in, n_all, res,
    load_sem, core_send, core_recv, xy_send, xy_recv, z_send, z_recv, ag_send, ag_recv,
    fw_send, fw_recv, pair_send, pair_recv, cross_send, cross_recv, back_send, back_recv, out_sem,
):
    rank, rows = p_t.shape
    nt = nx * ny
    hrank = rank // CORES
    crank = hrank // nx
    width = rows // ny
    quarter = rank // 4
    npair = nz // 2

    dp, t = lax.axis_index("dp"), lax.axis_index("tensor")
    z, c = lax.div(dp, CORES), lax.rem(dp, CORES)
    x, y = lax.div(t, ny), lax.rem(t, ny)

    def device(z_at, c_at, x_at, y_at):
        return {"dp": z_at * CORES + c_at, "tensor": x_at * ny + y_at}

    def around(at, step, n):
        return lax.rem(at + step, n)

    def send(src, dst, send_sem, recv_sem, to):
        pltpu.make_async_remote_copy(
            src_ref=src, dst_ref=dst, send_sem=send_sem, recv_sem=recv_sem,
            device_id=to, device_id_type=MESH,
        ).start()

    sibling = device(z, 1 - c, x, y)
    plane = sorted(
        ((dx, dy) for dx in range(nx) for dy in range(ny) if dx or dy),
        key=lambda d: -(min(d[0], nx - d[0]) + min(d[1], ny - d[1])),
    )
    ring = ring_order(nz)
    mate = z + 1 - 2 * lax.rem(z, 2)

    block_order = ring_order(ny) + [0]

    def columns(offset):
        return pl.ds(pl.multiple_of(around(y, offset, ny) * width, width), width)

    loads = [
        [pltpu.make_async_copy(grad_hbm, grads, load_sem.at[0]),
         pltpu.make_async_copy(q_hbm, q_prev, load_sem.at[1])]
    ]
    for k, offset in enumerate(block_order):
        at = columns(offset)
        loads.append([
            pltpu.make_async_copy(act_hbm.at[:, at], act.at[:, at], load_sem.at[2 + 2 * k]),
            pltpu.make_async_copy(err_hbm.at[0, at, :], err.at[at, :], load_sem.at[3 + 2 * k]),
        ])
    for group in loads:
        for copy in group:
            copy.start()

    barrier = pltpu.get_barrier_semaphore()
    greeted = [sibling, device(mate, 1 - c, x, y)]
    greeted += [device(z, c, around(x, dx, nx), around(y, dy, ny)) for dx, dy in plane]
    greeted += [device(around(z, dz, nz), c, x, y) for dz in ring]
    for other in greeted:
        pl.semaphore_signal(barrier, inc=1, device_id=other, device_id_type=MESH)

    own_half = pl.ds(pl.multiple_of(c * hrank, hrank), hrank)
    other_half = pl.ds(pl.multiple_of((1 - c) * hrank, hrank), hrank)

    def scatter(k, offset):
        at = columns(offset)
        await_bytes(from_core.at[k], core_recv.at[k])
        half[k] = part[own_half, at] + from_core[k]
        for dx in ring_order(nx) + [0]:
            to_x = around(x, dx, nx)
            mine = pl.ds(pl.multiple_of(to_x * crank, crank), crank)
            if dx == 0 and offset == 0:
                xy_in[t] = half[k, mine, :]
            else:
                send(half.at[k, mine, :], xy_in.at[t], xy_send, xy_recv,
                     device(z, c, to_x, around(y, offset, ny)))

    for copy in loads[0]:
        copy.wait()
    q_split = split(q_prev[...])
    for k, offset in enumerate(block_order):
        at = columns(offset)
        for copy in loads[1 + k]:
            copy.wait()
        block = dot(act[:, at], grads[...], 0, 0) + err[at, :]
        merged[at, :] = block
        part[:, at] = dot3(q_split, split(block), 1, 1)
        if k == 0:
            pl.semaphore_wait(barrier, len(greeted))
        send(part.at[other_half, at], from_core.at[k], core_send, core_recv.at[k], sibling)
        if k > 0:
            scatter(k - 1, block_order[k - 1])
    scatter(ny - 1, block_order[-1])

    await_bytes(xy_in.at[pl.ds(0, nt - 1)], xy_recv)
    piece = jnp.sum(xy_in[...], axis=0)
    z_out[...] = piece
    for dz in ring:
        send(z_out, z_in.at[z], z_send, z_recv, device(around(z, dz, nz), c, x, y))
    z_in[z] = piece
    await_bytes(z_in.at[pl.ds(0, nz - 1)], z_recv)
    my_rows = pl.ds(pl.multiple_of(c * hrank + x * crank, crank), crank)
    my_piece = p_t.at[my_rows, columns(0)]
    my_piece[...] = jnp.sum(z_in[...], axis=0)

    for dx, dy in plane:
        send(my_piece, my_piece, ag_send, ag_recv.at[(ny - dy) % ny],
             device(z, c, around(x, dx, nx), around(y, dy, ny)))
    near_first = list(reversed(block_order))
    for offset in near_first:
        count = (nx - 1 if offset == 0 else nx) * crank
        await_bytes(p_t.at[pl.ds(0, count), pl.ds(0, width)], ag_recv.at[offset])
        piece_ref = p_t.at[own_half, columns(offset)]
        send(piece_ref, piece_ref, fw_send, fw_recv.at[offset], sibling)
    total = None
    for offset in near_first:
        at = columns(offset)
        await_bytes(p_t.at[pl.ds(0, hrank), pl.ds(0, width)], fw_recv.at[offset])
        term = dot3(split(p_t[:, at]), split(merged[at, :]), 1, 0)
        total = term if total is None else total + term
    n_own[...] = total

    place = lax.rem(z, 2) * CORES + c

    def rows_of(at):
        return pl.ds(pl.multiple_of(at * quarter, quarter), quarter)

    group = [(mate, 1 - c), (mate, c), (z, 1 - c)]
    for z_at, c_at in group:
        there = lax.rem(z_at, 2) * CORES + c_at
        send(n_own.at[rows_of(there), :], pair_in.at[place], pair_send, pair_recv,
             device(z_at, c_at, x, y))
    pair_in[place] = n_own[rows_of(place), :]

    gram = dot(p_t[...], p_t[...], 1, 1, highest)
    row_at = lax.broadcasted_iota(jnp.int32, (rank, rank), 0)
    col_at = lax.broadcasted_iota(jnp.int32, (rank, rank), 1)
    eye = jnp.where(row_at == col_at, 1.0, 0.0).astype(f32)
    trace = jnp.sum(jnp.sum(gram * eye, axis=1, keepdims=True), axis=0, keepdims=True)
    shift = ridge_scale * rows * (trace / (rows * rank) + 1e-05)
    both = jnp.concatenate([gram + shift * eye, eye], axis=1)
    rank_at = lax.broadcasted_iota(jnp.int32, (rank, 1), 0)

    def eliminate(table, pivots, first, last):
        for k in range(first, last):
            pivot = table[k : k + 1, k : k + 1]
            pivots = jnp.where(rank_at == k, pivot, pivots)
            scale = jnp.where(rank_at > k, table[:, k : k + 1] * (1.0 / pivot), 0.0)
            table = table - scale * table[k : k + 1, :]
        return table, pivots

    early = rank // 4
    both, pivots = eliminate(both, jnp.ones((rank, 1), f32), 0, early)

    await_bytes(pair_in.at[pl.ds(0, 3)], pair_recv)
    piece = jnp.sum(pair_in[...], axis=0)
    cross_out[...] = piece
    pair_at = lax.div(z, 2)
    for dz in ring:
        if dz % 2 == 0:
            send(cross_out, cross_in.at[pair_at], cross_send, cross_recv,
                 device(around(z, dz, nz), c, x, y))
    cross_in[pair_at] = piece

    both, pivots = eliminate(both, pivots, early, rank)
    inverse = both[:, rank:] * (1.0 / jnp.sqrt(pivots))

    await_bytes(cross_in.at[pl.ds(0, npair - 1)], cross_recv)
    mine = n_all.at[rows_of(place), :]
    mine[...] = jnp.sum(cross_in[...], axis=0)
    for z_at, c_at in group:
        send(mine, mine, back_send, back_recv, device(z_at, c_at, x, y))
    await_bytes(n_all.at[pl.ds(0, 3 * quarter), :], back_recv)

    factor = dot(inverse, n_all[...], 1, 0, highest) * (1.0 / (nz * CORES))
    factor_ref[...] = factor
    back = split(dot(inverse, factor, 0, 0, highest))
    outs = []
    for offset in near_first:
        at = columns(offset)
        res[at, :] = merged[at, :] - dot3(split(p_t[:, at].T), back, 1, 0)
        outs.append(pltpu.make_async_copy(res.at[at, :], res_hbm.at[0, at, :], out_sem.at[offset]))
        outs[-1].start()

    await_bytes(from_core, core_send)
    await_bytes(xy_in.at[pl.ds(0, nt - 1)], xy_send)
    await_bytes(z_in.at[pl.ds(0, nz - 1)], z_send)
    await_bytes(xy_in.at[pl.ds(0, nt - 1)], ag_send)
    await_bytes(from_core, fw_send)
    await_bytes(pair_in.at[pl.ds(0, 3)], pair_send)
    await_bytes(cross_in.at[pl.ds(0, npair - 1)], cross_send)
    await_bytes(pair_in.at[pl.ds(0, 3)], back_send)
    for copy in outs:
        copy.wait()


def on_device(nx, ny, nz, activations, out_grads, q_previous, carried_error):
    tokens, rows = activations.shape
    width = out_grads.shape[1]
    rank = q_previous.shape[0]
    nt = nx * ny
    piece = (rank // CORES // nx, rows // ny)
    quarter = (rank // 4, width)
    vmem, dma = pltpu.VMEM, pltpu.SemaphoreType.DMA
    anywhere = pl.BlockSpec(memory_space=pl.ANY)
    factor, residual = pl.pallas_call(
        functools.partial(kernel, nx, ny, nz),
        name="powersgd",
        out_shape=(
            jax.ShapeDtypeStruct((rank, width), f32),
            jax.ShapeDtypeStruct((1, rows, width), f32),
        ),
        in_specs=[anywhere] * 4,
        out_specs=(pl.BlockSpec(memory_space=pltpu.VMEM), anywhere),
        scratch_shapes=[
            vmem((tokens, rows), bf16),
            vmem((tokens, width), bf16),
            vmem((rank, width), f32),
            vmem((rows, width), f32),
            vmem((rows, width), f32),
            vmem((rank, rows), f32),
            vmem((ny, rank // CORES, rows // ny), f32),
            vmem((ny, rank // CORES, rows // ny), f32),
            vmem((nt, *piece), f32),
            vmem(piece, f32),
            vmem((nz, *piece), f32),
            vmem((rank, rows), f32),
            vmem((rank, width), f32),
            vmem((4, *quarter), f32),
            vmem(quarter, f32),
            vmem((nz // 2, *quarter), f32),
            vmem((rank, width), f32),
            vmem((rows, width), f32),
            dma((2 + 2 * ny,)),
            dma, dma((ny,)),
            dma, dma,
            dma, dma,
            dma, dma((ny,)),
            dma, dma((ny,)),
            dma, dma,
            dma, dma,
            dma, dma,
            dma((ny,)),
        ],
        compiler_params=pltpu.CompilerParams(
            collective_id=0, has_side_effects=True, vmem_limit_bytes=32 * 1024 * 1024
        ),
    )(activations, out_grads, q_previous, carried_error)
    return factor, residual


def solution(mesh):
    nz = mesh.shape["dp"] // CORES
    nx = ny = {16: 4, 4: 2}[mesh.shape["tensor"]]
    placed = (P("dp", None), P("dp", "tensor"), P(None, "tensor"), P("dp", None, "tensor"))
    return jax.shard_map(
        functools.partial(on_device, nx, ny, nz),
        mesh=mesh,
        in_specs=placed,
        out_specs=(P(None, "tensor"), P("dp", None, "tensor")),
        check_vma=False,
    )
```

time: 683 us -> 67.6 us (0.10)
  waiting for transfers between devices: 643 us -> 0 us
  Pallas kernels: 0 us -> 60.4 us
  between operations: 14.8 us -> 0.65 us
  other arithmetic: 12.9 us -> 0 us
  matrix products: 10.6 us -> 0 us
    psum x2 -> x0, waiting for transfers between devices: 643 us -> none  [the longest x1 462 us: on_device(): p_sum = lax.psum(partial_value, ('dp', 'tensor'))]
    pallas_call x0 -> x1, Pallas kernels: none -> 60.4 us  [on_device(): pl.pallas_call(functools.partial(kernel, nx, ny, nz), name='powersgd', ou...]
    another operation x5 -> x0, other arithmetic: 12.1 us -> none  [the longest x3 6.52 us: orthonormal(): jnp.linalg.cholesky(gram_matrix + ridge_shift * jnp.eye(rank_size, dtype=...]
    dot_general x5 -> x0, matrix products: 9.24 us -> none  [the longest x1 2.13 us: on_device(): lax.dot_general(activations, out_grads, (((0,), (0,)), ((), ())), preferr...]
  transfers between devices with their start and end apart: 2 -> 0, of which waited for: 2 -> 0; matrix products, arithmetic and copies ran while one was open for 0% -> 0% of each run, Pallas kernels for 0% -> 0%
where the time goes in v1:
time: 67.6 us; the launch traced here: 67.3 us
  Pallas kernels  60.4 us (89%)
  local copies, waits for them, and re-layouts  6.29 us (9%)
    pallas_call x1, Pallas kernels, on_device(): pl.pallas_call(functools.partial(kernel, nx, ny, nz), name='powersgd', ou...  60.4 us
    unnamed x10, local copies, waits for them, and re-layouts  6.29 us

profile of v1, /device:TPU:1, one launch (start us, length us, event | category | flops | bytes accessed | tf_op | source)
XLA Modules:
  0.0 67.3 jit_solution(1532286077569861799)
XLA Ops:
  0.6 0.0 copy-start
  0.6 1.6 %copy-done = bf16[1024,1024]{1,0:T(8,128)(2,1)S(1)} copy-done((bf16[1024,1024]{1,0:T(8,128)(2,1)S(1)}, bf16[1024,1024]{1,0:T(8,128)(2,1)}, u32[]{:S(2)}) %copy-start) | copy-done | bytes 2097176
  2.2 0.0 copy-start.1
  2.2 1.2 %copy-done.1 = f32[1,1024,256]{2,1,0:T(8,128)S(1)} copy-done((f32[1,1024,256]{2,1,0:T(8,128)S(1)}, f32[1,1024,256]{2,1,0:T(8,128)}, u32[]{:S(2)}) %copy-start.1) | copy-done | bytes 1048600
  3.4 0.0 copy-start.2
  3.5 1.0 %copy-done.2 = bf16[1024,256]{1,0:T(8,128)(2,1)S(1)} copy-done((bf16[1024,256]{1,0:T(8,128)(2,1)S(1)}, bf16[1024,256]{1,0:T(8,128)(2,1)}, u32[]{:S(2)}) %copy-start.2) | copy-done | bytes 524312
  4.5 0.0 copy-start.3
  4.5 0.8 %copy-done.3 = f32[64,256]{1,0:T(8,128)S(1)} copy-done((f32[64,256]{1,0:T(8,128)S(1)}, f32[64,256]{1,0:T(8,128)}, u32[]{:S(2)}) %copy-start.3) | copy-done | bytes 65560
  5.3 60.4 %powersgd.1 = (f32[64,256]{1,0:T(8,128)S(1)}, f32[1,1024,256]{2,1,0:T(8,128)S(1)}) custom-call(bf16[1024,1024]{1,0:T(8,128)(2,1)S(1)} %copy-done, bf16[1024,256]{1,0:T(8,128)(2,1)S(1)} %copy-done.2, f32[64,256]{1,0:T(8,128)S(1)} %copy-done.3, f32[1,1024,256]{2,1,0:T(8,128)S(1)} %copy-done.1), custom_call_target="tpu_custom_call" | custom-call | tf_op jit(solution)/shard_map/powersgd/pallas_call | solution.py:251
  65.7 0.6 copy.8
  66.3 1.0 %copy.9 = f32[1,1024,256]{2,1,0:T(8,128)} copy(f32[1,1024,256]{2,1,0:T(8,128)S(1)} %get-tuple-element.5) | data formatting | bytes 2097152
Async XLA Ops:
  0.6 1.6 %copy-start = (bf16[1024,1024]{1,0:T(8,128)(2,1)S(1)}, bf16[1024,1024]{1,0:T(8,128)(2,1)}, u32[]{:S(2)}) copy-start(bf16[1024,1024]{1,0:T(8,128)(2,1)} %act_hbm.1) | copy-start | bytes 6291460
  2.2 1.2 %copy-start.1 = (f32[1,1024,256]{2,1,0:T(8,128)S(1)}, f32[1,1024,256]{2,1,0:T(8,128)}, u32[]{:S(2)}) copy-start(f32[1,1024,256]{2,1,0:T(8,128)} %err_hbm.1) | copy-start | bytes 3145732
  3.4 1.0 %copy-start.2 = (bf16[1024,256]{1,0:T(8,128)(2,1)S(1)}, bf16[1024,256]{1,0:T(8,128)(2,1)}, u32[]{:S(2)}) copy-start(bf16[1024,256]{1,0:T(8,128)(2,1)} %grad_hbm.1) | copy-start | bytes 1572868
  4.5 0.8 %copy-start.3 = (f32[64,256]{1,0:T(8,128)S(1)}, f32[64,256]{1,0:T(8,128)}, u32[]{:S(2)}) copy-start(f32[64,256]{1,0:T(8,128)} %q_hbm.1) | copy-start | bytes 196612

commit v2 on v1

--- a/solution.py
+++ b/solution.py
@@ -42,9 +42,9 @@
     nx, ny, nz,
     act_hbm, grad_hbm, q_hbm, err_hbm, factor_ref, res_hbm,
     act, grads, q_prev, err, merged, part, from_core, half, xy_in, z_out, z_in, p_t,
-    n_own, pair_in, cross_out, cross_in, n_all, res,
-    load_sem, core_send, core_recv, xy_send, xy_recv, z_send, z_recv, ag_send, ag_recv,
-    fw_send, fw_recv, pair_send, pair_recv, cross_send, cross_recv, back_send, back_recv, out_sem,
+    n_own, pair_in, cross_out, cross_in, n_all, table, res,
+    load_sem, core_send, core_recv, xy_send, xy_recv, z_send, z_recv, ag_send, far_send, ag_recv,
+    fw_send, fw_recv, pair_send, pair_recv, cross_send, cross_recv, back_send, back_recv, out_sem, known,
 ):
     rank, rows = p_t.shape
     nt = nx * ny
@@ -98,9 +98,11 @@
             copy.start()
 
     barrier = pltpu.get_barrier_semaphore()
-    greeted = [sibling, device(mate, 1 - c, x, y)]
-    greeted += [device(z, c, around(x, dx, nx), around(y, dy, ny)) for dx, dy in plane]
-    greeted += [device(around(z, dz, nz), c, x, y) for dz in ring]
+    near = [dz for dz in ring if min(dz, nz - dz) <= nz // 4]
+    greeted = [device(z, c, around(x, dx, nx), around(y, dy, ny)) for dx, dy in plane]
+    greeted += [device(around(z, dz, nz), c, x, y) for dz in near]
+    greeted += [device(z, 1 - c, around(x, dx, nx), around(y, ny // 2, ny)) for dx in range(nx)]
+    greeted += [device(mate, 1 - c, x, y), sibling]
     for other in greeted:
         pl.semaphore_signal(barrier, inc=1, device_id=other, device_id_type=MESH)
 
@@ -122,16 +124,22 @@
 
     for copy in loads[0]:
         copy.wait()
-    q_split = split(q_prev[...])
+    q_both = jnp.concatenate(split(q_prev[...]), axis=0)
+    projected = dot(q_both, grads[...], 1, 1)
+    projected = jnp.concatenate(split(projected[:rank] + projected[rank:]), axis=0)
     for k, offset in enumerate(block_order):
         at = columns(offset)
         for copy in loads[1 + k]:
             copy.wait()
-        block = dot(act[:, at], grads[...], 0, 0) + err[at, :]
-        merged[at, :] = block
-        part[:, at] = dot3(q_split, split(block), 1, 1)
+        err_high, err_low = split(err[at, :])
+        term = dot(projected, act[:, at], 1, 0) + dot(q_both, err_high, 1, 1)
+        part[:, at] = (term[:rank] + term[rank:]) + dot(q_both[:rank], err_low, 1, 1)
         if k == 0:
             pl.semaphore_wait(barrier, len(greeted))
+            for dz in (nz // 4, nz - nz // 4):
+                pl.semaphore_signal(
+                    known, inc=1, device_id=device(around(z, dz, nz), c, x, y), device_id_type=MESH
+                )
         send(part.at[other_half, at], from_core.at[k], core_send, core_recv.at[k], sibling)
         if k > 0:
             scatter(k - 1, block_order[k - 1])
@@ -140,27 +148,43 @@
     await_bytes(xy_in.at[pl.ds(0, nt - 1)], xy_recv)
     piece = jnp.sum(xy_in[...], axis=0)
     z_out[...] = piece
+    pl.semaphore_wait(known, 2)
     for dz in ring:
         send(z_out, z_in.at[z], z_send, z_recv, device(around(z, dz, nz), c, x, y))
     z_in[z] = piece
+
+    def gradient(k, carry):
+        at = pl.ds(pl.multiple_of(k * width, width), width)
+        merged[at, :] = dot(act[:, at], grads[...], 0, 0) + err[at, :]
+        return carry
+
+    lax.fori_loop(0, ny, gradient, 0)
     await_bytes(z_in.at[pl.ds(0, nz - 1)], z_recv)
     my_rows = pl.ds(pl.multiple_of(c * hrank + x * crank, crank), crank)
     my_piece = p_t.at[my_rows, columns(0)]
     my_piece[...] = jnp.sum(z_in[...], axis=0)
 
+    far = ny // 2
     for dx, dy in plane:
         send(my_piece, my_piece, ag_send, ag_recv.at[(ny - dy) % ny],
              device(z, c, around(x, dx, nx), around(y, dy, ny)))
+        if dy == far:
+            send(my_piece, my_piece, far_send, ag_recv.at[far],
+                 device(z, 1 - c, around(x, dx, nx), around(y, far, ny)))
     near_first = list(reversed(block_order))
     for offset in near_first:
-        count = (nx - 1 if offset == 0 else nx) * crank
-        await_bytes(p_t.at[pl.ds(0, count), pl.ds(0, width)], ag_recv.at[offset])
-        piece_ref = p_t.at[own_half, columns(offset)]
-        send(piece_ref, piece_ref, fw_send, fw_recv.at[offset], sibling)
+        if offset != far:
+            count = (nx - 1 if offset == 0 else nx) * crank
+            await_bytes(p_t.at[pl.ds(0, count), pl.ds(0, width)], ag_recv.at[offset])
+            piece_ref = p_t.at[own_half, columns(offset)]
+            send(piece_ref, piece_ref, fw_send, fw_recv.at[offset], sibling)
     total = None
     for offset in near_first:
         at = columns(offset)
-        await_bytes(p_t.at[pl.ds(0, hrank), pl.ds(0, width)], fw_recv.at[offset])
+        if offset == far:
+            await_bytes(p_t.at[:, pl.ds(0, width)], ag_recv.at[far])
+        else:
+            await_bytes(p_t.at[pl.ds(0, hrank), pl.ds(0, width)], fw_recv.at[offset])
         term = dot3(split(p_t[:, at]), split(merged[at, :]), 1, 0)
         total = term if total is None else total + term
     n_own[...] = total
@@ -183,19 +207,22 @@
     eye = jnp.where(row_at == col_at, 1.0, 0.0).astype(f32)
     trace = jnp.sum(jnp.sum(gram * eye, axis=1, keepdims=True), axis=0, keepdims=True)
     shift = ridge_scale * rows * (trace / (rows * rank) + 1e-05)
-    both = jnp.concatenate([gram + shift * eye, eye], axis=1)
+    table[...] = jnp.concatenate([gram + shift * eye, eye], axis=1)
     rank_at = lax.broadcasted_iota(jnp.int32, (rank, 1), 0)
 
-    def eliminate(table, pivots, first, last):
-        for k in range(first, last):
-            pivot = table[k : k + 1, k : k + 1]
-            pivots = jnp.where(rank_at == k, pivot, pivots)
-            scale = jnp.where(rank_at > k, table[:, k : k + 1] * (1.0 / pivot), 0.0)
-            table = table - scale * table[k : k + 1, :]
-        return table, pivots
-
-    early = rank // 4
-    both, pivots = eliminate(both, jnp.ones((rank, 1), f32), 0, early)
+    def eliminate(first, last):
+        def step(k, held):
+            for j in range(8):
+                row = held[j : j + 1, :]
+                scale = held[:, j : j + 1] * (1.0 / row[:, j : j + 1])
+                held = held - jnp.where((rank_at > j) & (rank_at < rank - 8 * k), scale, 0.0) * row
+            held = jnp.concatenate([held[8:], held[:8]], axis=0)
+            return pltpu.roll(held, 2 * rank - 8, 1)
+
+        table[...] = lax.fori_loop(first, last, step, table[...])
+
+    early = rank // 32
+    eliminate(0, early)
 
     await_bytes(pair_in.at[pl.ds(0, 3)], pair_recv)
     piece = jnp.sum(pair_in[...], axis=0)
@@ -207,8 +234,9 @@
                  device(around(z, dz, nz), c, x, y))
     cross_in[pair_at] = piece
 
-    both, pivots = eliminate(both, pivots, early, rank)
-    inverse = both[:, rank:] * (1.0 / jnp.sqrt(pivots))
+    eliminate(early, rank // 8)
+    pivots = jnp.sum(table[:, rank:] * eye, axis=1, keepdims=True)
+    inverse = table[:, :rank] * (1.0 / jnp.sqrt(pivots))
 
     await_bytes(cross_in.at[pl.ds(0, npair - 1)], cross_recv)
     mine = n_all.at[rows_of(place), :]
@@ -231,7 +259,8 @@
     await_bytes(xy_in.at[pl.ds(0, nt - 1)], xy_send)
     await_bytes(z_in.at[pl.ds(0, nz - 1)], z_send)
     await_bytes(xy_in.at[pl.ds(0, nt - 1)], ag_send)
-    await_bytes(from_core, fw_send)
+    await_bytes(xy_in.at[pl.ds(0, nx)], far_send)
+    await_bytes(from_core.at[pl.ds(0, ny - 1)], fw_send)
     await_bytes(pair_in.at[pl.ds(0, 3)], pair_send)
     await_bytes(cross_in.at[pl.ds(0, npair - 1)], cross_send)
     await_bytes(pair_in.at[pl.ds(0, 3)], back_send)
@@ -275,20 +304,22 @@
             vmem(quarter, f32),
             vmem((nz // 2, *quarter), f32),
             vmem((rank, width), f32),
+            vmem((rank, 2 * rank), f32),
             vmem((rows, width), f32),
             dma((2 + 2 * ny,)),
             dma, dma((ny,)),
             dma, dma,
             dma, dma,
+            dma, dma, dma((ny,)),
             dma, dma((ny,)),
-            dma, dma((ny,)),
             dma, dma,
             dma, dma,
             dma, dma,
             dma((ny,)),
+            pltpu.SemaphoreType.REGULAR,
         ],
         compiler_params=pltpu.CompilerParams(
-            collective_id=0, has_side_effects=True, vmem_limit_bytes=32 * 1024 * 1024
+            collective_id=0, has_side_effects=True
         ),
     )(activations, out_grads, q_previous, carried_error)
     return factor, residual

time: 67.6 us -> 59.3 us (0.88)
  Pallas kernels: 60.4 us -> 54.7 us
  local copies, waits for them, and re-layouts: 6.29 us -> 3.73 us
    pallas_call x1, Pallas kernels: 60.4 us -> 54.7 us  [on_device(): pl.pallas_call(functools.partial(kernel, nx, ny, nz), name='powersgd', ou...]
    unnamed x10 -> x2, local copies, waits for them, and re-layouts: 6.29 us -> 3.73 us
where the time goes in v2:
time: 59.3 us; the launch traced here: 59.1 us
  Pallas kernels  54.7 us (92%)
  local copies, waits for them, and re-layouts  3.73 us (6%)
  between operations  0.64 us (1%)
    pallas_call x1, Pallas kernels, on_device(): pl.pallas_call(functools.partial(kernel, nx, ny, nz), name='powersgd', ou...  54.7 us
    unnamed x2, local copies, waits for them, and re-layouts  3.73 us

profile of v2, /device:TPU:1, one launch (start us, length us, event | category | flops | bytes accessed | tf_op | source)
XLA Modules:
  0.0 59.1 jit_solution(14558786082246652234)
XLA Ops:
  0.6 54.7 %powersgd.1 = (f32[64,256]{1,0:T(8,128)}, f32[1,1024,256]{2,1,0:T(8,128)}) custom-call(bf16[1024,1024]{1,0:T(8,128)(2,1)} %act_hbm.1, bf16[1024,256]{1,0:T(8,128)(2,1)} %grad_hbm.1, f32[64,256]{1,0:T(8,128)} %q_hbm.1, f32[1,1024,256]{2,1,0:T(8,128)} %err_hbm.1), custom_call_target="tpu_custom_call" | custom-call | tf_op jit(solution)/shard_map/powersgd/pallas_call | solution.py:280
  55.3 1.5 %copy.8 = f32[64,256]{1,0:T(8,128)} copy(f32[64,256]{1,0:T(8,128)} %get-tuple-element.4) | data formatting | bytes 131072
  56.8 2.3 %copy.9 = f32[1,1024,256]{2,1,0:T(8,128)} copy(f32[1,1024,256]{2,1,0:T(8,128)} %get-tuple-element.5) | data formatting | bytes 2097152

commit v3 on v2

--- a/solution.py
+++ b/solution.py
@@ -40,11 +40,11 @@
 
 def kernel(
     nx, ny, nz,
-    act_hbm, grad_hbm, q_hbm, err_hbm, factor_ref, res_hbm,
-    act, grads, q_prev, err, merged, part, from_core, half, xy_in, z_out, z_in, p_t,
-    n_own, pair_in, cross_out, cross_in, n_all, table, res,
+    act_hbm, grad_hbm, q_hbm, err_hbm, merged, p_t, n_all, inverse,
+    act, grads, q_prev, err, part, from_core, half, xy_in, z_out, z_in,
+    n_own, pair_in, cross_out, cross_in, table,
     load_sem, core_send, core_recv, xy_send, xy_recv, z_send, z_recv, ag_send, far_send, ag_recv,
-    fw_send, fw_recv, pair_send, pair_recv, cross_send, cross_recv, back_send, back_recv, out_sem, known,
+    fw_send, fw_recv, pair_send, pair_recv, cross_send, cross_recv, back_send, back_recv, known,
 ):
     rank, rows = p_t.shape
     nt = nx * ny
@@ -236,7 +236,7 @@
 
     eliminate(early, rank // 8)
     pivots = jnp.sum(table[:, rank:] * eye, axis=1, keepdims=True)
-    inverse = table[:, :rank] * (1.0 / jnp.sqrt(pivots))
+    inverse[...] = table[:, :rank] * (1.0 / jnp.sqrt(pivots))
 
     await_bytes(cross_in.at[pl.ds(0, npair - 1)], cross_recv)
     mine = n_all.at[rows_of(place), :]
@@ -244,16 +244,6 @@
     for z_at, c_at in group:
         send(mine, mine, back_send, back_recv, device(z_at, c_at, x, y))
     await_bytes(n_all.at[pl.ds(0, 3 * quarter), :], back_recv)
-
-    factor = dot(inverse, n_all[...], 1, 0, highest) * (1.0 / (nz * CORES))
-    factor_ref[...] = factor
-    back = split(dot(inverse, factor, 0, 0, highest))
-    outs = []
-    for offset in near_first:
-        at = columns(offset)
-        res[at, :] = merged[at, :] - dot3(split(p_t[:, at].T), back, 1, 0)
-        outs.append(pltpu.make_async_copy(res.at[at, :], res_hbm.at[0, at, :], out_sem.at[offset]))
-        outs[-1].start()
 
     await_bytes(from_core, core_send)
     await_bytes(xy_in.at[pl.ds(0, nt - 1)], xy_send)
@@ -264,8 +254,23 @@
     await_bytes(pair_in.at[pl.ds(0, 3)], pair_send)
     await_bytes(cross_in.at[pl.ds(0, npair - 1)], cross_send)
     await_bytes(pair_in.at[pl.ds(0, 3)], back_send)
-    for copy in outs:
-        copy.wait()
+
+
+def finish(replicas, merged, p_t, n_all, inverse, factor_hbm, res_hbm, factor, res, sems):
+    rows = merged.shape[0]
+    factor[...] = dot(inverse[...], n_all[...], 1, 0, highest) * (1.0 / replicas)
+    out = pltpu.make_async_copy(factor, factor_hbm, sems.at[0])
+    out.start()
+    outs = [out]
+    back = split(dot(inverse[...], factor[...], 0, 0, highest))
+    step = rows // 4
+    for k in range(4):
+        at = pl.ds(k * step, step)
+        res[at, :] = merged[at, :] - dot3(split(p_t[:, at].T), back, 1, 0)
+        outs.append(pltpu.make_async_copy(res.at[at, :], res_hbm.at[0, at, :], sems.at[1 + k]))
+        outs[-1].start()
+    for out in outs:
+        out.wait()
 
 
 def on_device(nx, ny, nz, activations, out_grads, q_previous, carried_error):
@@ -277,20 +282,26 @@
     quarter = (rank // 4, width)
     vmem, dma = pltpu.VMEM, pltpu.SemaphoreType.DMA
     anywhere = pl.BlockSpec(memory_space=pl.ANY)
-    factor, residual = pl.pallas_call(
+    in_hbm = [
+        pltpu.with_memory_space_constraint(a, pltpu.HBM)
+        for a in (activations, out_grads, q_previous, carried_error)
+    ]
+    local = pl.BlockSpec(memory_space=pltpu.VMEM)
+    passed = pl.pallas_call(
         functools.partial(kernel, nx, ny, nz),
         name="powersgd",
         out_shape=(
-            jax.ShapeDtypeStruct((rank, width), f32),
-            jax.ShapeDtypeStruct((1, rows, width), f32),
+            vmem((rows, width), f32),
+            vmem((rank, rows), f32),
+            vmem((rank, width), f32),
+            vmem((rank, rank), f32),
         ),
         in_specs=[anywhere] * 4,
-        out_specs=(pl.BlockSpec(memory_space=pltpu.VMEM), anywhere),
+        out_specs=(local,) * 4,
         scratch_shapes=[
             vmem((tokens, rows), bf16),
             vmem((tokens, width), bf16),
             vmem((rank, width), f32),
-            vmem((rows, width), f32),
             vmem((rows, width), f32),
             vmem((rank, rows), f32),
             vmem((ny, rank // CORES, rows // ny), f32),
@@ -298,14 +309,11 @@
             vmem((nt, *piece), f32),
             vmem(piece, f32),
             vmem((nz, *piece), f32),
-            vmem((rank, rows), f32),
             vmem((rank, width), f32),
             vmem((4, *quarter), f32),
             vmem(quarter, f32),
             vmem((nz // 2, *quarter), f32),
-            vmem((rank, width), f32),
             vmem((rank, 2 * rank), f32),
-            vmem((rows, width), f32),
             dma((2 + 2 * ny,)),
             dma, dma((ny,)),
             dma, dma,
@@ -315,14 +323,24 @@
             dma, dma,
             dma, dma,
             dma, dma,
-            dma((ny,)),
             pltpu.SemaphoreType.REGULAR,
         ],
         compiler_params=pltpu.CompilerParams(
-            collective_id=0, has_side_effects=True
+            collective_id=0, has_side_effects=True, vmem_limit_bytes=16 * 1024 * 1024
         ),
-    )(activations, out_grads, q_previous, carried_error)
-    return factor, residual
+    )(*in_hbm)
+    return pl.pallas_call(
+        functools.partial(finish, nz * CORES),
+        name="residual",
+        out_shape=(
+            jax.ShapeDtypeStruct((rank, width), f32),
+            jax.ShapeDtypeStruct((1, rows, width), f32),
+        ),
+        in_specs=[local] * 4,
+        out_specs=(anywhere,) * 2,
+        scratch_shapes=[vmem((rank, width), f32), vmem((rows, width), f32), dma((5,))],
+        compiler_params=pltpu.CompilerParams(vmem_limit_bytes=16 * 1024 * 1024),
+    )(*(pltpu.with_memory_space_constraint(a, pltpu.VMEM) for a in passed))
 
 
 def solution(mesh):

time: 59.3 us -> 54.8 us (0.924)
  local copies, waits for them, and re-layouts: 3.73 us -> 0 us
  Pallas kernels: 54.7 us -> 54.1 us
    unnamed x2 -> x0, local copies, waits for them, and re-layouts: 3.73 us -> none
    pallas_call x1, Pallas kernels: 54.7 us -> 52.2 us  [on_device(): pl.pallas_call(functools.partial(kernel, nx, ny, nz), name='powersgd', ou...]
    pallas_call x0 -> x1, Pallas kernels: none -> 1.85 us  [on_device(): pl.pallas_call(functools.partial(finish, nz * CORES), name='residual', ou...]
where the time goes in v3:
time: 54.8 us; the launch traced here: 54.7 us
  Pallas kernels  54.1 us (99%)
  between operations  0.64 us (1%)
    pallas_call x1, Pallas kernels, on_device(): pl.pallas_call(functools.partial(kernel, nx, ny, nz), name='powersgd', ou...  52.2 us
    pallas_call x1, Pallas kernels, on_device(): pl.pallas_call(functools.partial(finish, nz * CORES), name='residual', ou...  1.85 us

profile of v3, /device:TPU:1, one launch (start us, length us, event | category | flops | bytes accessed | tf_op | source)
XLA Modules:
  0.0 54.7 jit_solution(1299937871596433774)
XLA Ops:
  0.6 52.2 %powersgd.1 = (f32[1024,256]{1,0:T(8,128)S(1)}, f32[64,1024]{1,0:T(8,128)S(1)}, f32[64,256]{1,0:T(8,128)S(1)}, f32[64,64]{1,0:T(8,128)S(1)}) custom-call(bf16[1024,1024]{1,0:T(8,128)(2,1)} %act_hbm.1, bf16[1024,256]{1,0:T(8,128)(2,1)} %grad_hbm.1, f32[64,256]{1,0:T(8,128)} %q_hbm.1, f32[1,1024,256]{2,1,0:T(8,128)} %err_hbm.1), custom_call_target="tpu_custom_call" | custom-call | tf_op jit(solution)/shard_map/powersgd/pallas_call | solution.py:290
  52.9 1.9 %residual.1 = (f32[64,256]{1,0:T(8,128)}, f32[1,1024,256]{2,1,0:T(8,128)}) custom-call(f32[1024,256]{1,0:T(8,128)S(1)} %get-tuple-element.6.merged, f32[64,1024]{1,0:T(8,128)S(1)} %get-tuple-element.7.p_t, f32[64,256]{1,0:T(8,128)S(1)} %get-tuple-element.8.n_all, f32[64,64]{1,0:T(8,128)S(1)} %get-tuple-element.9.inverse), custom_call_target="tpu_custom_call" | custom-call | tf_op jit(solution)/shard_map/residual/pallas_call | solution.py:332

commit v4 on v3

v4 whole, which is shorter than its diff:
```python
import functools

import jax
import jax.numpy as jnp
from jax import lax
from jax.experimental import pallas as pl
from jax.experimental.pallas import tpu as pltpu
from jax.sharding import PartitionSpec as P

ridge_scale = 0.001
highest = lax.Precision.HIGHEST
f32 = jnp.float32
bf16 = jnp.bfloat16
MESH = pl.DeviceIdType.MESH
CORES = 2


def dot(a, b, ca, cb, precision=None):
    return lax.dot_general(
        a, b, (((ca,), (cb,)), ((), ())), precision=precision, preferred_element_type=f32
    )


def split(value):
    high = value.astype(bf16)
    return high, (value - high.astype(f32)).astype(bf16)


def dot3(a, b, ca, cb):
    return dot(a[0], b[0], ca, cb) + (dot(a[0], b[1], ca, cb) + dot(a[1], b[0], ca, cb))


def await_bytes(ref, sem):
    pltpu.make_async_copy(ref, ref, sem).wait()


def ring_order(n):
    return sorted(range(1, n), key=lambda k: -min(k, n - k))


def kernel(
    nx, ny, nz,
    act_hbm, grad_hbm, q_hbm, err_hbm, merged, basis, n_all, inverse,
    act, grads, q_prev, err, part, from_core, half, xy_in, z_out, z_in, p_t,
    packed, m_core, m_out, m_own, m_mate, m_high, m_low, cross_out, cross_in, table,
    load_sem, core_send, core_recv, xy_send, xy_recv, z_send, z_recv, ag_send, ag_recv,
    fw_send, fw_recv, pack_send, pack_recv, mate_send, mate_recv,
    cross_send, cross_recv, back_send, back_recv, known,
):
    rank, rows = p_t.shape
    width = merged.shape[1]
    nt = nx * ny
    half_rows = rows // CORES
    block = half_rows // 2
    prank, pcols = rank // nx, half_rows // ny
    npair = nz // 2
    ncol = width // 4

    dp, t = lax.axis_index("dp"), lax.axis_index("tensor")
    z, c = lax.div(dp, CORES), lax.rem(dp, CORES)
    x, y = lax.div(t, ny), lax.rem(t, ny)
    odd = lax.rem(z, 2)
    mate = z + 1 - 2 * odd

    def device(z_at, c_at, x_at, y_at):
        return {"dp": z_at * CORES + c_at, "tensor": x_at * ny + y_at}

    def around(at, step, n):
        return lax.rem(at + step, n)

    def span(start, size):
        return pl.ds(pl.multiple_of(start, size), size)

    def send(src, dst, send_sem, recv_sem, to):
        pltpu.make_async_remote_copy(
            src_ref=src, dst_ref=dst, send_sem=send_sem, recv_sem=recv_sem,
            device_id=to, device_id_type=MESH,
        ).start()

    sibling = device(z, 1 - c, x, y)
    plane = sorted(
        ((dx, dy) for dx in range(nx) for dy in range(ny) if dx or dy),
        key=lambda d: -(min(d[0], nx - d[0]) + min(d[1], ny - d[1])),
    )
    ring = ring_order(nz)

    loads = [
        [pltpu.make_async_copy(grad_hbm, grads, load_sem.at[0]),
         pltpu.make_async_copy(q_hbm, q_prev, load_sem.at[1])]
    ]
    starts = [h * half_rows + j * block for h in (1 - c, c) for j in range(2)]
    for k, start in enumerate(starts):
        at = span(start, block)
        loads.append([
            pltpu.make_async_copy(act_hbm.at[:, at], act.at[:, at], load_sem.at[2 + 2 * k]),
            pltpu.make_async_copy(err_hbm.at[0, at, :], err.at[at, :], load_sem.at[3 + 2 * k]),
        ])
    for group in loads:
        for copy in group:
            copy.start()

    barrier = pltpu.get_barrier_semaphore()
    near = [dz for dz in ring if min(dz, nz - dz) <= nz // 4]
    greeted = [device(z, c, around(x, dx, nx), around(y, dy, ny)) for dx, dy in plane]
    greeted += [device(around(z, dz, nz), c, x, y) for dz in near]
    greeted += [device(mate, 1 - c, x, y), sibling]
    for other in greeted:
        pl.semaphore_signal(barrier, inc=1, device_id=other, device_id_type=MESH)

    for copy in loads[0]:
        copy.wait()
    q_both = jnp.concatenate(split(q_prev[...]), axis=0)
    projected = dot(q_both, grads[...], 1, 1)
    projected = jnp.concatenate(split(projected[:rank] + projected[rank:]), axis=0)
    for k, start in enumerate(starts):
        at = span(start, block)
        for copy in loads[1 + k]:
            copy.wait()
        err_high, err_low = split(err[at, :])
        term = dot(projected, act[:, at], 1, 0) + dot(q_both, err_high, 1, 1)
        part[:, at] = (term[:rank] + term[rank:]) + dot(q_both[:rank], err_low, 1, 1)
        if k == 1:
            pl.semaphore_wait(barrier, len(greeted))
            send(part.at[:, span((1 - c) * half_rows, half_rows)], from_core,
                 core_send, core_recv, sibling)
            for dz in (nz // 4, nz - nz // 4):
                pl.semaphore_signal(
                    known, inc=1, device_id=device(around(z, dz, nz), c, x, y), device_id_type=MESH
                )

    own_half = span(c * half_rows, half_rows)
    await_bytes(from_core, core_recv)
    half[...] = part[:, own_half] + from_core[...]

    def piece_of(ref, x_at, y_at):
        return ref.at[span(x_at * prank, prank), span(y_at * pcols, pcols)]

    for dx, dy in plane:
        x_at, y_at = around(x, dx, nx), around(y, dy, ny)
        send(piece_of(half, x_at, y_at), xy_in.at[t], xy_send, xy_recv, device(z, c, x_at, y_at))
    xy_in[t] = piece_of(half, x, y)[...]

    def gradient(k, carry):
        top_at, low_at = span(k * block, block), span(half_rows + k * block, block)
        top = dot(act[:, top_at], grads[...], 0, 0) + err[top_at, :]
        low = dot(act[:, low_at], grads[...], 0, 0) + err[low_at, :]
        merged[top_at, :] = top
        merged[low_at, :] = low
        for core in range(CORES):
            for parity in range(2):
                at = (parity * CORES + core) * ncol
                packed[core, parity, top_at, :] = jnp.concatenate(
                    [top[:, at : at + ncol], low[:, at : at + ncol]], axis=1
                )
        return carry

    lax.fori_loop(0, 2, gradient, 0)
    send(packed.at[1 - c], m_core, pack_send, pack_recv, sibling)

    await_bytes(xy_in.at[pl.ds(0, nt - 1)], xy_recv)
    piece = jnp.sum(xy_in[...], axis=0)
    z_out[...] = piece
    pl.semaphore_wait(known, 2)
    for dz in ring:
        send(z_out, z_in.at[z], z_send, z_recv, device(around(z, dz, nz), c, x, y))
    z_in[z] = piece

    await_bytes(m_core, pack_recv)
    m_out[...] = packed[c, 1 - odd] + m_core[1 - odd]
    send(m_out, m_mate, mate_send, mate_recv, device(mate, c, x, y))
    m_own[...] = packed[c, odd] + m_core[odd]

    await_bytes(z_in.at[pl.ds(0, nz - 1)], z_recv)

    def mine_of(x_at, y_at):
        return p_t.at[span(x_at * prank, prank), span(c * half_rows + y_at * pcols, pcols)]

    my_piece = mine_of(x, y)
    my_piece[...] = jnp.sum(z_in[...], axis=0)

    for dx, dy in plane:
        send(my_piece, my_piece, ag_send, ag_recv.at[(ny - dy) % ny],
             device(z, c, around(x, dx, nx), around(y, dy, ny)))
    await_bytes(m_mate, mate_recv)
    m_high[...], m_low[...] = split(m_own[...] + m_mate[...])
    near_first = [0] + list(reversed(ring_order(ny)))
    for offset in near_first:
        count = (nx - 1 if offset == 0 else nx) * prank
        await_bytes(p_t.at[pl.ds(0, count), pl.ds(0, pcols)], ag_recv.at[offset])
        ready = p_t.at[:, span(c * half_rows + around(y, offset, ny) * pcols, pcols)]
        send(ready, ready, fw_send, fw_recv.at[offset], sibling)

    total = jnp.zeros((2 * rank, 2 * ncol), f32)
    for offset in near_first:
        await_bytes(p_t.at[:, pl.ds(0, pcols)], fw_recv.at[offset])
        first = around(y, offset, ny) * pcols
        at = span(first, pcols)
        both = jnp.concatenate([p_t[:, at], p_t[:, span(half_rows + first, pcols)]], axis=0)
        total += dot3(split(both), (m_high[at, :], m_low[at, :]), 1, 0)
    terms = total[:rank, :ncol] + total[rank:, ncol:]
    terms = jnp.concatenate([terms[: rank // 2], terms[rank // 2 :]], axis=1)
    cross_out[...] = terms

    pair_at = lax.div(z, 2)
    for dz in ring:
        if dz % 2 == 0:
            send(cross_out, cross_in.at[pair_at], cross_send, cross_recv,
                 device(around(z, dz, nz), c, x, y))
    cross_in[pair_at] = terms

    gram = dot(p_t[...], p_t[...], 1, 1, highest)
    row_at = lax.broadcasted_iota(jnp.int32, (rank, rank), 0)
    col_at = lax.broadcasted_iota(jnp.int32, (rank, rank), 1)
    eye = jnp.where(row_at == col_at, 1.0, 0.0).astype(f32)
    trace = jnp.sum(jnp.sum(gram * eye, axis=1, keepdims=True), axis=0, keepdims=True)
    shift = ridge_scale * rows * (trace / (rows * rank) + 1e-05)
    table[...] = jnp.concatenate([gram + shift * eye, eye], axis=1)
    rank_at = lax.broadcasted_iota(jnp.int32, (rank, 1), 0)

    def eliminate(k, held):
        for j in range(8):
            row = held[j : j + 1, :]
            scale = held[:, j : j + 1] * (1.0 / row[:, j : j + 1])
            held = held - jnp.where((rank_at > j) & (rank_at < rank - 8 * k), scale, 0.0) * row
        held = jnp.concatenate([held[8:], held[:8]], axis=0)
        return pltpu.roll(held, 2 * rank - 8, 1)

    table[...] = lax.fori_loop(0, rank // 8, eliminate, table[...])

    await_bytes(cross_in.at[pl.ds(0, npair - 1)], cross_recv)
    place = odd * CORES + c
    n_all[place] = jnp.sum(cross_in[...], axis=0)
    for z_at, c_at in ((mate, 1 - c), (mate, c), (z, 1 - c)):
        send(n_all.at[place], n_all.at[place], back_send, back_recv, device(z_at, c_at, x, y))

    pivots = jnp.sum(table[:, rank:] * eye, axis=1, keepdims=True)
    inverse[...] = table[:, :rank] * (1.0 / jnp.sqrt(pivots))

    def transposed(k, carry):
        at = span(k * block, block)
        high, low = split(p_t[:, at].T)
        basis[at, :] = jnp.concatenate([high, low, high, jnp.zeros_like(high)], axis=1)
        return carry

    lax.fori_loop(0, rows // block, transposed, 0)

    await_bytes(n_all.at[pl.ds(0, 3)], back_recv)
    await_bytes(from_core, core_send)
    await_bytes(xy_in.at[pl.ds(0, nt - 1)], xy_send)
    await_bytes(m_core, pack_send)
    await_bytes(z_in.at[pl.ds(0, nz - 1)], z_send)
    await_bytes(m_mate, mate_send)
    await_bytes(xy_in.at[pl.ds(0, nt - 1)], ag_send)
    await_bytes(from_core, fw_send)
    await_bytes(cross_in.at[pl.ds(0, npair - 1)], cross_send)
    await_bytes(n_all.at[pl.ds(0, 3)], back_send)


def finish(replicas, merged, basis, n_all, inverse, factor_hbm, res_hbm, factor, res, sems):
    rows = merged.shape[0]
    ncol = n_all.shape[2] // 2
    top = jnp.concatenate([n_all[k][:, :ncol] for k in range(4)], axis=1)
    low = jnp.concatenate([n_all[k][:, ncol:] for k in range(4)], axis=1)
    terms = jnp.concatenate([top, low], axis=0)
    factor[...] = dot(inverse[...], terms, 1, 0, highest) * (1.0 / replicas)
    out = pltpu.make_async_copy(factor, factor_hbm, sems.at[0])
    out.start()
    outs = [out]
    high, low = split(dot(inverse[...], factor[...], 0, 0, highest))
    back = jnp.concatenate([high, high, low, jnp.zeros_like(low)], axis=0)
    step = rows // 4
    for k in range(4):
        at = pl.ds(k * step, step)
        res[at, :] = merged[at, :] - dot(basis[at, :], back, 1, 0)
        outs.append(pltpu.make_async_copy(res.at[at, :], res_hbm.at[0, at, :], sems.at[1 + k]))
        outs[-1].start()
    for out in outs:
        out.wait()


def on_device(nx, ny, nz, activations, out_grads, q_previous, carried_error):
    tokens, rows = activations.shape
    width = out_grads.shape[1]
    rank = q_previous.shape[0]
    half_rows = rows // CORES
    piece = (rank // nx, half_rows // ny)
    columns = (half_rows, width // 2)
    terms = (rank // 2, width // 2)
    vmem, dma = pltpu.VMEM, pltpu.SemaphoreType.DMA
    anywhere = pl.BlockSpec(memory_space=pl.ANY)
    local = pl.BlockSpec(memory_space=pltpu.VMEM)
    in_hbm = [
        pltpu.with_memory_space_constraint(a, pltpu.HBM)
        for a in (activations, out_grads, q_previous, carried_error)
    ]
    passed = pl.pallas_call(
        functools.partial(kernel, nx, ny, nz),
        name="powersgd",
        out_shape=(
            vmem((rows, width), f32),
            vmem((rows, 4 * rank), bf16),
            vmem((4, *terms), f32),
            vmem((rank, rank), f32),
        ),
        in_specs=[anywhere] * 4,
        out_specs=(local,) * 4,
        scratch_shapes=[
            vmem((tokens, rows), bf16),
            vmem((tokens, width), bf16),
            vmem((rank, width), f32),
            vmem((rows, width), f32),
            vmem((rank, rows), f32),
            vmem((rank, half_rows), f32),
            vmem((rank, half_rows), f32),
            vmem((nx * ny, *piece), f32),
            vmem(piece, f32),
            vmem((nz, *piece), f32),
            vmem((rank, rows), f32),
            vmem((CORES, 2, *columns), f32),
            vmem((2, *columns), f32),
            vmem(columns, f32),
            vmem(columns, f32),
            vmem(columns, f32),
            vmem(columns, bf16),
            vmem(columns, bf16),
            vmem(terms, f32),
            vmem((nz // 2, *terms), f32),
            vmem((rank, 2 * rank), f32),
            dma((10,)),
            dma, dma,
            dma, dma,
            dma, dma,
            dma, dma((ny,)),
            dma, dma((ny,)),
            dma, dma,
            dma, dma,
            dma, dma,
            dma, dma,
            pltpu.SemaphoreType.REGULAR,
        ],
        compiler_params=pltpu.CompilerParams(
            collective_id=0, has_side_effects=True, vmem_limit_bytes=20 * 1024 * 1024
        ),
    )(*in_hbm)
    return pl.pallas_call(
        functools.partial(finish, nz * CORES),
        name="residual",
        out_shape=(
            jax.ShapeDtypeStruct((rank, width), f32),
            jax.ShapeDtypeStruct((1, rows, width), f32),
        ),
        in_specs=[local] * 4,
        out_specs=(anywhere,) * 2,
        scratch_shapes=[vmem((rank, width), f32), vmem((rows, width), f32), dma((5,))],
        compiler_params=pltpu.CompilerParams(vmem_limit_bytes=16 * 1024 * 1024),
    )(*(pltpu.with_memory_space_constraint(a, pltpu.VMEM) for a in passed))


def solution(mesh):
    nz = mesh.shape["dp"] // CORES
    nx = ny = {16: 4, 4: 2}[mesh.shape["tensor"]]
    placed = (P("dp", None), P("dp", "tensor"), P(None, "tensor"), P("dp", None, "tensor"))
    return jax.shard_map(
        functools.partial(on_device, nx, ny, nz),
        mesh=mesh,
        in_specs=placed,
        out_specs=(P(None, "tensor"), P("dp", None, "tensor")),
        check_vma=False,
    )
```

time: 54.8 us -> 51.3 us (0.936)
  Pallas kernels: 54.1 us -> 50.5 us
    pallas_call x1, Pallas kernels: 52.2 us -> 48.8 us  [on_device(): pl.pallas_call(functools.partial(kernel, nx, ny, nz), name='powersgd', ou...]
where the time goes in v4:
time: 51.3 us; the launch traced here: 51.2 us
  Pallas kernels  50.5 us (98%)
  between operations  0.64 us (1%)
    pallas_call x1, Pallas kernels, on_device(): pl.pallas_call(functools.partial(kernel, nx, ny, nz), name='powersgd', ou...  48.8 us
    pallas_call x1, Pallas kernels, on_device(): pl.pallas_call(functools.partial(finish, nz * CORES), name='residual', ou...  1.74 us

profile of v4, /device:TPU:1, one launch (start us, length us, event | category | flops | bytes accessed | tf_op | source)
XLA Modules:
  0.0 51.2 jit_solution(3749555461615056547)
XLA Ops:
  0.6 48.8 %powersgd.1 = (f32[1024,256]{1,0:T(8,128)S(1)}, bf16[1024,256]{1,0:T(8,128)(2,1)S(1)}, f32[4,32,128]{2,1,0:T(8,128)S(1)}, f32[64,64]{1,0:T(8,128)S(1)}) custom-call(bf16[1024,1024]{1,0:T(8,128)(2,1)} %act_hbm.1, bf16[1024,256]{1,0:T(8,128)(2,1)} %grad_hbm.1, f32[64,256]{1,0:T(8,128)} %q_hbm.1, f32[1,1024,256]{2,1,0:T(8,128)} %err_hbm.1), custom_call_target="tpu_custom_call" | custom-call | tf_op jit(solution)/shard_map/powersgd/pallas_call | solution.py:296
  49.4 1.7 %residual.1 = (f32[64,256]{1,0:T(8,128)}, f32[1,1024,256]{2,1,0:T(8,128)}) custom-call(f32[1024,256]{1,0:T(8,128)S(1)} %get-tuple-element.6.merged, bf16[1024,256]{1,0:T(8,128)(2,1)S(1)} %get-tuple-element.7.basis, f32[4,32,128]{2,1,0:T(8,128)S(1)} %get-tuple-element.8.n_all, f32[64,64]{1,0:T(8,128)S(1)} %get-tuple-element.9.inverse), custom_call_target="tpu_custom_call" | custom-call | tf_op jit(solution)/shard_map/residual/pallas_call | solution.py:345

commit v5 on v4

--- a/solution.py
+++ b/solution.py
@@ -13,6 +13,7 @@
 bf16 = jnp.bfloat16
 MESH = pl.DeviceIdType.MESH
 CORES = 2
+FAR = {4: 5, 2: 1}
 
 
 def dot(a, b, ca, cb, precision=None):
@@ -42,19 +43,20 @@
     nx, ny, nz,
     act_hbm, grad_hbm, q_hbm, err_hbm, merged, basis, n_all, inverse,
     act, grads, q_prev, err, part, from_core, half, xy_in, z_out, z_in, p_t,
-    packed, m_core, m_out, m_own, m_mate, m_high, m_low, cross_out, cross_in, table,
+    m_core, m_out, m_mate, m_pair, cross_out, cross_in, table,
     load_sem, core_send, core_recv, xy_send, xy_recv, z_send, z_recv, ag_send, ag_recv,
-    fw_send, fw_recv, pack_send, pack_recv, mate_send, mate_recv,
+    fw_send, fw_recv, m_send, m_recv, mate_send, mate_recv, pair_send, pair_recv,
     cross_send, cross_recv, back_send, back_recv, known,
 ):
     rank, rows = p_t.shape
     width = merged.shape[1]
     nt = nx * ny
     half_rows = rows // CORES
-    block = half_rows // 2
-    prank, pcols = rank // nx, half_rows // ny
+    half_rank = rank // CORES
+    block = rows // 4
+    prank, pcols = half_rank // nx, rows // ny
     npair = nz // 2
-    ncol = width // 4
+    half_width = width // 2
 
     dp, t = lax.axis_index("dp"), lax.axis_index("tensor")
     z, c = lax.div(dp, CORES), lax.rem(dp, CORES)
@@ -82,82 +84,101 @@
         ((dx, dy) for dx in range(nx) for dy in range(ny) if dx or dy),
         key=lambda d: -(min(d[0], nx - d[0]) + min(d[1], ny - d[1])),
     )
+    far = [d for d in plane if min(d[0], nx - d[0]) + min(d[1], ny - d[1]) > nx // 2]
+    near_plane = [d for d in plane if d not in far]
     ring = ring_order(nz)
 
     loads = [
         [pltpu.make_async_copy(grad_hbm, grads, load_sem.at[0]),
          pltpu.make_async_copy(q_hbm, q_prev, load_sem.at[1])]
     ]
-    starts = [h * half_rows + j * block for h in (1 - c, c) for j in range(2)]
-    for k, start in enumerate(starts):
-        at = span(start, block)
+    for k in range(4):
+        at = pl.ds(k * block, block)
         loads.append([
             pltpu.make_async_copy(act_hbm.at[:, at], act.at[:, at], load_sem.at[2 + 2 * k]),
             pltpu.make_async_copy(err_hbm.at[0, at, :], err.at[at, :], load_sem.at[3 + 2 * k]),
         ])
+    barrier = pltpu.get_barrier_semaphore()
+    near = [dz for dz in ring if min(dz, nz - dz) <= nz // 4]
+    greeted = [
+        (min(dx, nx - dx) + min(dy, ny - dy), device(z, c, around(x, dx, nx), around(y, dy, ny)))
+        for dx, dy in plane
+    ]
+    greeted += [(min(dz, nz - dz), device(around(z, dz, nz), c, x, y)) for dz in near]
+    greeted += [
+        (min(dx, nx - dx) + min(dy, ny - dy), device(z, 1 - c, around(x, dx, nx), around(y, dy, ny)))
+        for dx, dy in far
+    ]
+    greeted += [(1, device(mate, 1 - c, x, y)), (0, sibling)]
+    for _, other in sorted(greeted, key=lambda pair: -pair[0]):
+        pl.semaphore_signal(barrier, inc=1, device_id=other, device_id_type=MESH)
     for group in loads:
         for copy in group:
             copy.start()
 
-    barrier = pltpu.get_barrier_semaphore()
-    near = [dz for dz in ring if min(dz, nz - dz) <= nz // 4]
-    greeted = [device(z, c, around(x, dx, nx), around(y, dy, ny)) for dx, dy in plane]
-    greeted += [device(around(z, dz, nz), c, x, y) for dz in near]
-    greeted += [device(mate, 1 - c, x, y), sibling]
-    for other in greeted:
-        pl.semaphore_signal(barrier, inc=1, device_id=other, device_id_type=MESH)
+    def gradient(k, carry):
+        at = span(k * block, block)
+        merged[at, :] = dot(act[:, at], grads[...], 0, 0) + err[at, :]
+        return carry
 
     for copy in loads[0]:
         copy.wait()
     q_both = jnp.concatenate(split(q_prev[...]), axis=0)
     projected = dot(q_both, grads[...], 1, 1)
     projected = jnp.concatenate(split(projected[:rank] + projected[rank:]), axis=0)
-    for k, start in enumerate(starts):
-        at = span(start, block)
+    for k in range(4):
+        at = pl.ds(k * block, block)
         for copy in loads[1 + k]:
             copy.wait()
         err_high, err_low = split(err[at, :])
         term = dot(projected, act[:, at], 1, 0) + dot(q_both, err_high, 1, 1)
         part[:, at] = (term[:rank] + term[rank:]) + dot(q_both[:rank], err_low, 1, 1)
-        if k == 1:
-            pl.semaphore_wait(barrier, len(greeted))
-            send(part.at[:, span((1 - c) * half_rows, half_rows)], from_core,
-                 core_send, core_recv, sibling)
-            for dz in (nz // 4, nz - nz // 4):
-                pl.semaphore_signal(
-                    known, inc=1, device_id=device(around(z, dz, nz), c, x, y), device_id_type=MESH
-                )
-
-    own_half = span(c * half_rows, half_rows)
+
+    pl.semaphore_wait(barrier, len(greeted))
+
+    own_ranks = span(c * half_rank, half_rank)
+    for k, (dx, dy) in enumerate(far):
+        x_at, y_at = around(x, dx, nx), around(y, dy, ny)
+        for c_at, slot in ((c, 0), (1 - c, 1)):
+            rows_at = span(c_at * half_rank + x_at * prank, prank)
+            send(part.at[rows_at, span(y_at * pcols, pcols)], xy_in.at[2 * k + slot],
+                 xy_send, xy_recv, device(z, c_at, x_at, y_at))
+    send(part.at[span((1 - c) * half_rank, half_rank), :], from_core, core_send, core_recv, sibling)
+    for dz in (nz // 4, nz - nz // 4):
+        pl.semaphore_signal(
+            known, inc=1, device_id=device(around(z, dz, nz), c, x, y), device_id_type=MESH
+        )
     await_bytes(from_core, core_recv)
-    half[...] = part[:, own_half] + from_core[...]
+    half[...] = part[own_ranks, :] + from_core[...]
 
     def piece_of(ref, x_at, y_at):
         return ref.at[span(x_at * prank, prank), span(y_at * pcols, pcols)]
 
-    for dx, dy in plane:
+    for k, (dx, dy) in enumerate(near_plane):
         x_at, y_at = around(x, dx, nx), around(y, dy, ny)
-        send(piece_of(half, x_at, y_at), xy_in.at[t], xy_send, xy_recv, device(z, c, x_at, y_at))
-    xy_in[t] = piece_of(half, x, y)[...]
-
-    def gradient(k, carry):
-        top_at, low_at = span(k * block, block), span(half_rows + k * block, block)
-        top = dot(act[:, top_at], grads[...], 0, 0) + err[top_at, :]
-        low = dot(act[:, low_at], grads[...], 0, 0) + err[low_at, :]
-        merged[top_at, :] = top
-        merged[low_at, :] = low
-        for core in range(CORES):
-            for parity in range(2):
-                at = (parity * CORES + core) * ncol
-                packed[core, parity, top_at, :] = jnp.concatenate(
-                    [top[:, at : at + ncol], low[:, at : at + ncol]], axis=1
-                )
-        return carry
-
-    lax.fori_loop(0, 2, gradient, 0)
-    send(packed.at[1 - c], m_core, pack_send, pack_recv, sibling)
-
-    await_bytes(xy_in.at[pl.ds(0, nt - 1)], xy_recv)
+        send(piece_of(half, x_at, y_at), xy_in.at[2 * len(far) + k],
+             xy_send, xy_recv, device(z, c, x_at, y_at))
+    arriving = nt - 1 + len(far)
+    xy_in[arriving] = piece_of(half, x, y)[...]
+
+    lax.fori_loop(0, 4, gradient, 0)
+    own_rows = span(c * half_rows, half_rows)
+    send(merged.at[span((1 - c) * half_rows, half_rows), :], m_core, m_send, m_recv, sibling)
+
+    def to_mate():
+        await_bytes(m_core, m_recv)
+        there = span((1 - odd) * half_width, half_width)
+        m_out[...] = merged[own_rows, there] + m_core[:, there]
+        send(m_out, m_mate, mate_send, mate_recv, device(mate, c, x, y))
+        here = span(odd * half_width, half_width)
+        m_pair[own_rows, :] = merged[own_rows, here] + m_core[:, here]
+
+    def to_sibling():
+        await_bytes(m_mate, mate_recv)
+        m_pair[own_rows, :] += m_mate[...]
+        send(m_pair.at[own_rows, :], m_pair.at[own_rows, :], pair_send, pair_recv, sibling)
+
+    await_bytes(xy_in.at[pl.ds(0, arriving)], xy_recv)
     piece = jnp.sum(xy_in[...], axis=0)
     z_out[...] = piece
     pl.semaphore_wait(known, 2)
@@ -165,40 +186,27 @@
         send(z_out, z_in.at[z], z_send, z_recv, device(around(z, dz, nz), c, x, y))
     z_in[z] = piece
 
-    await_bytes(m_core, pack_recv)
-    m_out[...] = packed[c, 1 - odd] + m_core[1 - odd]
-    send(m_out, m_mate, mate_send, mate_recv, device(mate, c, x, y))
-    m_own[...] = packed[c, odd] + m_core[odd]
-
+    to_mate()
     await_bytes(z_in.at[pl.ds(0, nz - 1)], z_recv)
 
-    def mine_of(x_at, y_at):
-        return p_t.at[span(x_at * prank, prank), span(c * half_rows + y_at * pcols, pcols)]
-
-    my_piece = mine_of(x, y)
+    my_piece = p_t.at[span(c * half_rank + x * prank, prank), span(y * pcols, pcols)]
     my_piece[...] = jnp.sum(z_in[...], axis=0)
 
     for dx, dy in plane:
         send(my_piece, my_piece, ag_send, ag_recv.at[(ny - dy) % ny],
              device(z, c, around(x, dx, nx), around(y, dy, ny)))
-    await_bytes(m_mate, mate_recv)
-    m_high[...], m_low[...] = split(m_own[...] + m_mate[...])
+    to_sibling()
+    await_bytes(m_pair.at[pl.ds(0, half_rows), :], pair_recv)
     near_first = [0] + list(reversed(ring_order(ny)))
+    terms = None
     for offset in near_first:
         count = (nx - 1 if offset == 0 else nx) * prank
         await_bytes(p_t.at[pl.ds(0, count), pl.ds(0, pcols)], ag_recv.at[offset])
-        ready = p_t.at[:, span(c * half_rows + around(y, offset, ny) * pcols, pcols)]
-        send(ready, ready, fw_send, fw_recv.at[offset], sibling)
-
-    total = jnp.zeros((2 * rank, 2 * ncol), f32)
-    for offset in near_first:
-        await_bytes(p_t.at[:, pl.ds(0, pcols)], fw_recv.at[offset])
-        first = around(y, offset, ny) * pcols
-        at = span(first, pcols)
-        both = jnp.concatenate([p_t[:, at], p_t[:, span(half_rows + first, pcols)]], axis=0)
-        total += dot3(split(both), (m_high[at, :], m_low[at, :]), 1, 0)
-    terms = total[:rank, :ncol] + total[rank:, ncol:]
-    terms = jnp.concatenate([terms[: rank // 2], terms[rank // 2 :]], axis=1)
+        at = span(around(y, offset, ny) * pcols, pcols)
+        ready = p_t.at[own_ranks, at]
+        send(ready, ready, fw_send, fw_recv, sibling)
+        term = dot3(split(ready[...]), split(m_pair[at, :]), 1, 0)
+        terms = term if terms is None else terms + term
     cross_out[...] = terms
 
     pair_at = lax.div(z, 2)
@@ -208,6 +216,7 @@
                  device(around(z, dz, nz), c, x, y))
     cross_in[pair_at] = terms
 
+    await_bytes(from_core, fw_recv)
     gram = dot(p_t[...], p_t[...], 1, 1, highest)
     row_at = lax.broadcasted_iota(jnp.int32, (rank, rank), 0)
     col_at = lax.broadcasted_iota(jnp.int32, (rank, rank), 1)
@@ -246,10 +255,11 @@
 
     await_bytes(n_all.at[pl.ds(0, 3)], back_recv)
     await_bytes(from_core, core_send)
-    await_bytes(xy_in.at[pl.ds(0, nt - 1)], xy_send)
-    await_bytes(m_core, pack_send)
+    await_bytes(xy_in.at[pl.ds(0, arriving)], xy_send)
+    await_bytes(m_core, m_send)
     await_bytes(z_in.at[pl.ds(0, nz - 1)], z_send)
     await_bytes(m_mate, mate_send)
+    await_bytes(m_pair.at[pl.ds(0, half_rows), :], pair_send)
     await_bytes(xy_in.at[pl.ds(0, nt - 1)], ag_send)
     await_bytes(from_core, fw_send)
     await_bytes(cross_in.at[pl.ds(0, npair - 1)], cross_send)
@@ -258,10 +268,9 @@
 
 def finish(replicas, merged, basis, n_all, inverse, factor_hbm, res_hbm, factor, res, sems):
     rows = merged.shape[0]
-    ncol = n_all.shape[2] // 2
-    top = jnp.concatenate([n_all[k][:, :ncol] for k in range(4)], axis=1)
-    low = jnp.concatenate([n_all[k][:, ncol:] for k in range(4)], axis=1)
-    terms = jnp.concatenate([top, low], axis=0)
+    terms = jnp.concatenate([
+        jnp.concatenate([n_all[k], n_all[CORES + k]], axis=1) for k in range(CORES)
+    ], axis=0)
     factor[...] = dot(inverse[...], terms, 1, 0, highest) * (1.0 / replicas)
     out = pltpu.make_async_copy(factor, factor_hbm, sems.at[0])
     out.start()
@@ -283,9 +292,10 @@
     width = out_grads.shape[1]
     rank = q_previous.shape[0]
     half_rows = rows // CORES
-    piece = (rank // nx, half_rows // ny)
-    columns = (half_rows, width // 2)
-    terms = (rank // 2, width // 2)
+    half_rank, half_width = rank // CORES, width // 2
+    piece = (half_rank // nx, rows // ny)
+    columns = (half_rows, half_width)
+    terms = (half_rank, half_width)
     vmem, dma = pltpu.VMEM, pltpu.SemaphoreType.DMA
     anywhere = pl.BlockSpec(memory_space=pl.ANY)
     local = pl.BlockSpec(memory_space=pltpu.VMEM)
@@ -310,19 +320,16 @@
             vmem((rank, width), f32),
             vmem((rows, width), f32),
             vmem((rank, rows), f32),
-            vmem((rank, half_rows), f32),
-            vmem((rank, half_rows), f32),
-            vmem((nx * ny, *piece), f32),
+            vmem((half_rank, rows), f32),
+            vmem((half_rank, rows), f32),
+            vmem((nx * ny + FAR[nx], *piece), f32),
             vmem(piece, f32),
             vmem((nz, *piece), f32),
             vmem((rank, rows), f32),
-            vmem((CORES, 2, *columns), f32),
-            vmem((2, *columns), f32),
+            vmem((half_rows, width), f32),
             vmem(columns, f32),
             vmem(columns, f32),
-            vmem(columns, f32),
-            vmem(columns, bf16),
-            vmem(columns, bf16),
+            vmem((rows, half_width), f32),
             vmem(terms, f32),
             vmem((nz // 2, *terms), f32),
             vmem((rank, 2 * rank), f32),
@@ -331,7 +338,8 @@
             dma, dma,
             dma, dma,
             dma, dma((ny,)),
-            dma, dma((ny,)),
+            dma, dma,
+            dma, dma,
             dma, dma,
             dma, dma,
             dma, dma,

time: 51.3 us -> 50.3 us (0.981)
  Pallas kernels: 50.5 us -> 49.6 us
    pallas_call x1, Pallas kernels: 48.8 us -> 47.9 us  [on_device(): pl.pallas_call(functools.partial(kernel, nx, ny, nz), name='powersgd', ou...]
where the time goes in v5:
time: 50.3 us; the launch traced here: 50.2 us
  Pallas kernels  49.6 us (99%)
  between operations  0.64 us (1%)
    pallas_call x1, Pallas kernels, on_device(): pl.pallas_call(functools.partial(kernel, nx, ny, nz), name='powersgd', ou...  47.9 us
    pallas_call x1, Pallas kernels, on_device(): pl.pallas_call(functools.partial(finish, nz * CORES), name='residual', ou...  1.66 us

profile of v5, /device:TPU:1, one launch (start us, length us, event | category | flops | bytes accessed | tf_op | source)
XLA Modules:
  0.0 50.2 jit_solution(3675893632948932653)
XLA Ops:
  0.6 47.9 %powersgd.1 = (f32[1024,256]{1,0:T(8,128)S(1)}, bf16[1024,256]{1,0:T(8,128)(2,1)S(1)}, f32[4,32,128]{2,1,0:T(8,128)S(1)}, f32[64,64]{1,0:T(8,128)S(1)}) custom-call(bf16[1024,1024]{1,0:T(8,128)(2,1)} %act_hbm.1, bf16[1024,256]{1,0:T(8,128)(2,1)} %grad_hbm.1, f32[64,256]{1,0:T(8,128)} %q_hbm.1, f32[1,1024,256]{2,1,0:T(8,128)} %err_hbm.1), custom_call_target="tpu_custom_call" | custom-call | tf_op jit(solution)/shard_map/powersgd/pallas_call | solution.py:306
  48.6 1.7 %residual.1 = (f32[64,256]{1,0:T(8,128)}, f32[1,1024,256]{2,1,0:T(8,128)}) custom-call(f32[1024,256]{1,0:T(8,128)S(1)} %get-tuple-element.6.merged, bf16[1024,256]{1,0:T(8,128)(2,1)S(1)} %get-tuple-element.7.basis, f32[4,32,128]{2,1,0:T(8,128)S(1)} %get-tuple-element.8.n_all, f32[64,64]{1,0:T(8,128)S(1)} %get-tuple-element.9.inverse), custom_call_target="tpu_custom_call" | custom-call | tf_op jit(solution)/shard_map/residual/pallas_call | solution.py:353

commit v6 on v5

--- a/solution.py
+++ b/solution.py
@@ -110,11 +110,21 @@
         for dx, dy in far
     ]
     greeted += [(1, device(mate, 1 - c, x, y)), (0, sibling)]
-    for _, other in sorted(greeted, key=lambda pair: -pair[0]):
-        pl.semaphore_signal(barrier, inc=1, device_id=other, device_id_type=MESH)
-    for group in loads:
-        for copy in group:
-            copy.start()
+    greeted.sort(key=lambda pair: -pair[0])
+
+    def start(groups):
+        for group in groups:
+            for copy in group:
+                copy.start()
+
+    def greet(others):
+        for other in others:
+            pl.semaphore_signal(barrier, inc=1, device_id=other, device_id_type=MESH)
+
+    start(loads[:2])
+    greet([other for hops, other in greeted if hops > 2])
+    start(loads[2:])
+    greet([other for hops, other in greeted if hops <= 2])
 
     def gradient(k, carry):
         at = span(k * block, block)
@@ -137,13 +147,13 @@
     pl.semaphore_wait(barrier, len(greeted))
 
     own_ranks = span(c * half_rank, half_rank)
+    send(part.at[span((1 - c) * half_rank, half_rank), :], from_core, core_send, core_recv, sibling)
     for k, (dx, dy) in enumerate(far):
         x_at, y_at = around(x, dx, nx), around(y, dy, ny)
         for c_at, slot in ((c, 0), (1 - c, 1)):
             rows_at = span(c_at * half_rank + x_at * prank, prank)
             send(part.at[rows_at, span(y_at * pcols, pcols)], xy_in.at[2 * k + slot],
                  xy_send, xy_recv, device(z, c_at, x_at, y_at))
-    send(part.at[span((1 - c) * half_rank, half_rank), :], from_core, core_send, core_recv, sibling)
     for dz in (nz // 4, nz - nz // 4):
         pl.semaphore_signal(
             known, inc=1, device_id=device(around(z, dz, nz), c, x, y), device_id_type=MESH
@@ -224,13 +234,30 @@
     trace = jnp.sum(jnp.sum(gram * eye, axis=1, keepdims=True), axis=0, keepdims=True)
     shift = ridge_scale * rows * (trace / (rows * rank) + 1e-05)
     table[...] = jnp.concatenate([gram + shift * eye, eye], axis=1)
-    rank_at = lax.broadcasted_iota(jnp.int32, (rank, 1), 0)
+    rank_at = lax.broadcasted_iota(jnp.int32, (rank, 2 * rank), 0)
 
     def eliminate(k, held):
-        for j in range(8):
-            row = held[j : j + 1, :]
-            scale = held[:, j : j + 1] * (1.0 / row[:, j : j + 1])
-            held = held - jnp.where((rank_at > j) & (rank_at < rank - 8 * k), scale, 0.0) * row
+        for j in range(0, 8, 4):
+            lines = [held[j + i : j + i + 1, :] for i in range(4)]
+            square = [
+                [jnp.broadcast_to(line[:, j + r : j + r + 1], line.shape) for r in range(4)]
+                for line in lines
+            ]
+            scales = [jnp.broadcast_to(held[:, j + i : j + i + 1], held.shape) for i in range(4)]
+            change = None
+            for i in range(4):
+                inv = 1.0 / square[i][i]
+                below = (rank_at > j + i) & (rank_at < rank - 8 * k)
+                scale = jnp.where(below, scales[i], 0.0)
+                term = scale * (lines[i] * inv)
+                change = term if change is None else change + term
+                for l in range(i + 1, 4):
+                    share = square[l][i] * inv
+                    lines[l] = lines[l] - share * lines[i]
+                    scales[l] = scales[l] - scale * (square[i][l] * inv)
+                    for r in range(i + 1, 4):
+                        square[l][r] = square[l][r] - share * square[i][r]
+            held = held - change
         held = jnp.concatenate([held[8:], held[:8]], axis=0)
         return pltpu.roll(held, 2 * rank - 8, 1)
 

time: 50.3 us -> 51.4 us (1.022)
  Pallas kernels: 49.6 us -> 50.6 us
    pallas_call x1, Pallas kernels: 47.9 us -> 48.9 us  [on_device(): pl.pallas_call(functools.partial(kernel, nx, ny, nz), name='powersgd', ou...]
where the time goes in v6:
time: 51.4 us; the launch traced here: 51.2 us
  Pallas kernels  50.6 us (98%)
  between operations  0.64 us (1%)
    pallas_call x1, Pallas kernels, on_device(): pl.pallas_call(functools.partial(kernel, nx, ny, nz), name='powersgd', ou...  48.9 us
    pallas_call x1, Pallas kernels, on_device(): pl.pallas_call(functools.partial(finish, nz * CORES), name='residual', ou...  1.66 us

profile of v6, /device:TPU:1, one launch (start us, length us, event | category | flops | bytes accessed | tf_op | source)
XLA Modules:
  0.0 51.2 jit_solution(11759823894477083705)
XLA Ops:
  0.6 48.9 %powersgd.1 = (f32[1024,256]{1,0:T(8,128)S(1)}, bf16[1024,256]{1,0:T(8,128)(2,1)S(1)}, f32[4,32,128]{2,1,0:T(8,128)S(1)}, f32[64,64]{1,0:T(8,128)S(1)}) custom-call(bf16[1024,1024]{1,0:T(8,128)(2,1)} %act_hbm.1, bf16[1024,256]{1,0:T(8,128)(2,1)} %grad_hbm.1, f32[64,256]{1,0:T(8,128)} %q_hbm.1, f32[1,1024,256]{2,1,0:T(8,128)} %err_hbm.1), custom_call_target="tpu_custom_call" | custom-call | tf_op jit(solution)/shard_map/powersgd/pallas_call | solution.py:333
  49.6 1.7 %residual.1 = (f32[64,256]{1,0:T(8,128)}, f32[1,1024,256]{2,1,0:T(8,128)}) custom-call(f32[1024,256]{1,0:T(8,128)S(1)} %get-tuple-element.6.merged, bf16[1024,256]{1,0:T(8,128)(2,1)S(1)} %get-tuple-element.7.basis, f32[4,32,128]{2,1,0:T(8,128)S(1)} %get-tuple-element.8.n_all, f32[64,64]{1,0:T(8,128)S(1)} %get-tuple-element.9.inverse), custom_call_target="tpu_custom_call" | custom-call | tf_op jit(solution)/shard_map/residual/pallas_call | solution.py:380

commit v7 on v6

--- a/solution.py
+++ b/solution.py
@@ -112,24 +112,15 @@
     greeted += [(1, device(mate, 1 - c, x, y)), (0, sibling)]
     greeted.sort(key=lambda pair: -pair[0])
 
-    def start(groups):
-        for group in groups:
-            for copy in group:
-                copy.start()
-
-    def greet(others):
-        for other in others:
-            pl.semaphore_signal(barrier, inc=1, device_id=other, device_id_type=MESH)
-
-    start(loads[:2])
-    greet([other for hops, other in greeted if hops > 2])
-    start(loads[2:])
-    greet([other for hops, other in greeted if hops <= 2])
-
-    def gradient(k, carry):
-        at = span(k * block, block)
+    for _, other in greeted:
+        pl.semaphore_signal(barrier, inc=1, device_id=other, device_id_type=MESH)
+    for group in loads:
+        for copy in group:
+            copy.start()
+
+    def gradient(start):
+        at = span(start, block)
         merged[at, :] = dot(act[:, at], grads[...], 0, 0) + err[at, :]
-        return carry
 
     for copy in loads[0]:
         copy.wait()
@@ -158,6 +149,7 @@
         pl.semaphore_signal(
             known, inc=1, device_id=device(around(z, dz, nz), c, x, y), device_id_type=MESH
         )
+    gradient((1 - c) * half_rows)
     await_bytes(from_core, core_recv)
     half[...] = part[own_ranks, :] + from_core[...]
 
@@ -171,9 +163,11 @@
     arriving = nt - 1 + len(far)
     xy_in[arriving] = piece_of(half, x, y)[...]
 
-    lax.fori_loop(0, 4, gradient, 0)
+    gradient((1 - c) * half_rows + block)
     own_rows = span(c * half_rows, half_rows)
     send(merged.at[span((1 - c) * half_rows, half_rows), :], m_core, m_send, m_recv, sibling)
+    gradient(c * half_rows)
+    gradient(c * half_rows + block)
 
     def to_mate():
         await_bytes(m_core, m_recv)
@@ -294,22 +288,20 @@
 
 
 def finish(replicas, merged, basis, n_all, inverse, factor_hbm, res_hbm, factor, res, sems):
-    rows = merged.shape[0]
     terms = jnp.concatenate([
         jnp.concatenate([n_all[k], n_all[CORES + k]], axis=1) for k in range(CORES)
     ], axis=0)
-    factor[...] = dot(inverse[...], terms, 1, 0, highest) * (1.0 / replicas)
-    out = pltpu.make_async_copy(factor, factor_hbm, sems.at[0])
-    out.start()
-    outs = [out]
-    high, low = split(dot(inverse[...], factor[...], 0, 0, highest))
+    values = dot(inverse[...], terms, 1, 0, highest) * (1.0 / replicas)
+    factor[...] = values
+    high, low = split(dot(inverse[...], values, 0, 0, highest))
     back = jnp.concatenate([high, high, low, jnp.zeros_like(low)], axis=0)
-    step = rows // 4
-    for k in range(4):
-        at = pl.ds(k * step, step)
-        res[at, :] = merged[at, :] - dot(basis[at, :], back, 1, 0)
-        outs.append(pltpu.make_async_copy(res.at[at, :], res_hbm.at[0, at, :], sems.at[1 + k]))
-        outs[-1].start()
+    res[...] = merged[...] - dot(basis[...], back, 1, 0)
+    outs = [
+        pltpu.make_async_copy(res, res_hbm.at[0], sems.at[0]),
+        pltpu.make_async_copy(factor, factor_hbm, sems.at[1]),
+    ]
+    for out in outs:
+        out.start()
     for out in outs:
         out.wait()
 
@@ -386,7 +378,7 @@
         ),
         in_specs=[local] * 4,
         out_specs=(anywhere,) * 2,
-        scratch_shapes=[vmem((rank, width), f32), vmem((rows, width), f32), dma((5,))],
+        scratch_shapes=[vmem((rank, width), f32), vmem((rows, width), f32), dma((2,))],
         compiler_params=pltpu.CompilerParams(vmem_limit_bytes=16 * 1024 * 1024),
     )(*(pltpu.with_memory_space_constraint(a, pltpu.VMEM) for a in passed))
 

time: 51.4 us -> 50.3 us (0.979)
  Pallas kernels: 50.6 us -> 49.6 us
    pallas_call x1, Pallas kernels: 48.9 us -> 47.9 us  [on_device(): pl.pallas_call(functools.partial(kernel, nx, ny, nz), name='powersgd', ou...]
where the time goes in v7:
time: 50.3 us; the launch traced here: 50.2 us
  Pallas kernels  49.6 us (99%)
  between operations  0.64 us (1%)
    pallas_call x1, Pallas kernels, on_device(): pl.pallas_call(functools.partial(kernel, nx, ny, nz), name='powersgd', ou...  47.9 us
    pallas_call x1, Pallas kernels, on_device(): pl.pallas_call(functools.partial(finish, nz * CORES), name='residual', ou...  1.72 us

profile of v7, /device:TPU:1, one launch (start us, length us, event | category | flops | bytes accessed | tf_op | source)
XLA Modules:
  0.0 50.2 jit_solution(6792814799891318666)
XLA Ops:
  0.6 47.9 %powersgd.1 = (f32[1024,256]{1,0:T(8,128)S(1)}, bf16[1024,256]{1,0:T(8,128)(2,1)S(1)}, f32[4,32,128]{2,1,0:T(8,128)S(1)}, f32[64,64]{1,0:T(8,128)S(1)}) custom-call(bf16[1024,1024]{1,0:T(8,128)(2,1)} %act_hbm.1, bf16[1024,256]{1,0:T(8,128)(2,1)} %grad_hbm.1, f32[64,256]{1,0:T(8,128)} %q_hbm.1, f32[1,1024,256]{2,1,0:T(8,128)} %err_hbm.1), custom_call_target="tpu_custom_call" | custom-call | tf_op jit(solution)/shard_map/powersgd/pallas_call | solution.py:325
  48.5 1.7 %residual.1 = (f32[64,256]{1,0:T(8,128)}, f32[1,1024,256]{2,1,0:T(8,128)}) custom-call(f32[1024,256]{1,0:T(8,128)S(1)} %get-tuple-element.6.merged, bf16[1024,256]{1,0:T(8,128)(2,1)S(1)} %get-tuple-element.7.basis, f32[4,32,128]{2,1,0:T(8,128)S(1)} %get-tuple-element.8.n_all, f32[64,64]{1,0:T(8,128)S(1)} %get-tuple-element.9.inverse), custom_call_target="tpu_custom_call" | custom-call | tf_op jit(solution)/shard_map/residual/pallas_call | solution.py:372

commit v8 on v7

--- a/solution.py
+++ b/solution.py
@@ -110,17 +110,16 @@
         for dx, dy in far
     ]
     greeted += [(1, device(mate, 1 - c, x, y)), (0, sibling)]
-    greeted.sort(key=lambda pair: -pair[0])
-
-    for _, other in greeted:
+    for _, other in sorted(greeted, key=lambda pair: -pair[0]):
         pl.semaphore_signal(barrier, inc=1, device_id=other, device_id_type=MESH)
     for group in loads:
         for copy in group:
             copy.start()
 
-    def gradient(start):
-        at = span(start, block)
+    def gradient(k, carry):
+        at = span(k * block, block)
         merged[at, :] = dot(act[:, at], grads[...], 0, 0) + err[at, :]
+        return carry
 
     for copy in loads[0]:
         copy.wait()
@@ -138,18 +137,17 @@
     pl.semaphore_wait(barrier, len(greeted))
 
     own_ranks = span(c * half_rank, half_rank)
-    send(part.at[span((1 - c) * half_rank, half_rank), :], from_core, core_send, core_recv, sibling)
     for k, (dx, dy) in enumerate(far):
         x_at, y_at = around(x, dx, nx), around(y, dy, ny)
         for c_at, slot in ((c, 0), (1 - c, 1)):
             rows_at = span(c_at * half_rank + x_at * prank, prank)
             send(part.at[rows_at, span(y_at * pcols, pcols)], xy_in.at[2 * k + slot],
                  xy_send, xy_recv, device(z, c_at, x_at, y_at))
+    send(part.at[span((1 - c) * half_rank, half_rank), :], from_core, core_send, core_recv, sibling)
     for dz in (nz // 4, nz - nz // 4):
         pl.semaphore_signal(
             known, inc=1, device_id=device(around(z, dz, nz), c, x, y), device_id_type=MESH
         )
-    gradient((1 - c) * half_rows)
     await_bytes(from_core, core_recv)
     half[...] = part[own_ranks, :] + from_core[...]
 
@@ -163,11 +161,9 @@
     arriving = nt - 1 + len(far)
     xy_in[arriving] = piece_of(half, x, y)[...]
 
-    gradient((1 - c) * half_rows + block)
+    lax.fori_loop(0, 4, gradient, 0)
     own_rows = span(c * half_rows, half_rows)
     send(merged.at[span((1 - c) * half_rows, half_rows), :], m_core, m_send, m_recv, sibling)
-    gradient(c * half_rows)
-    gradient(c * half_rows + block)
 
     def to_mate():
         await_bytes(m_core, m_recv)
@@ -288,6 +284,7 @@
 
 
 def finish(replicas, merged, basis, n_all, inverse, factor_hbm, res_hbm, factor, res, sems):
+    rows = merged.shape[0]
     terms = jnp.concatenate([
         jnp.concatenate([n_all[k], n_all[CORES + k]], axis=1) for k in range(CORES)
     ], axis=0)
@@ -295,13 +292,15 @@
     factor[...] = values
     high, low = split(dot(inverse[...], values, 0, 0, highest))
     back = jnp.concatenate([high, high, low, jnp.zeros_like(low)], axis=0)
-    res[...] = merged[...] - dot(basis[...], back, 1, 0)
-    outs = [
-        pltpu.make_async_copy(res, res_hbm.at[0], sems.at[0]),
-        pltpu.make_async_copy(factor, factor_hbm, sems.at[1]),
-    ]
-    for out in outs:
-        out.start()
+    outs = []
+    step = rows // 2
+    for k in range(2):
+        at = pl.ds(k * step, step)
+        res[at, :] = merged[at, :] - dot(basis[at, :], back, 1, 0)
+        outs.append(pltpu.make_async_copy(res.at[at, :], res_hbm.at[0, at, :], sems.at[k]))
+        outs[-1].start()
+    outs.append(pltpu.make_async_copy(factor, factor_hbm, sems.at[2]))
+    outs[-1].start()
     for out in outs:
         out.wait()
 
@@ -378,7 +377,7 @@
         ),
         in_specs=[local] * 4,
         out_specs=(anywhere,) * 2,
-        scratch_shapes=[vmem((rank, width), f32), vmem((rows, width), f32), dma((2,))],
+        scratch_shapes=[vmem((rank, width), f32), vmem((rows, width), f32), dma((3,))],
         compiler_params=pltpu.CompilerParams(vmem_limit_bytes=16 * 1024 * 1024),
     )(*(pltpu.with_memory_space_constraint(a, pltpu.VMEM) for a in passed))
 

time: 50.3 us -> 50.4 us (level)
  no operation moved by 1% of the time
where the time goes in v8:
time: 50.4 us; the launch traced here: 50.3 us
  Pallas kernels  49.7 us (99%)
  between operations  0.64 us (1%)
    pallas_call x1, Pallas kernels, on_device(): pl.pallas_call(functools.partial(kernel, nx, ny, nz), name='powersgd', ou...  47.9 us
    pallas_call x1, Pallas kernels, on_device(): pl.pallas_call(functools.partial(finish, nz * CORES), name='residual', ou...  1.73 us

profile of v8, /device:TPU:1, one launch (start us, length us, event | category | flops | bytes accessed | tf_op | source)
XLA Modules:
  0.0 50.3 jit_solution(4648035399646472049)
XLA Ops:
  0.6 47.9 %powersgd.1 = (f32[1024,256]{1,0:T(8,128)S(1)}, bf16[1024,256]{1,0:T(8,128)(2,1)S(1)}, f32[4,32,128]{2,1,0:T(8,128)S(1)}, f32[64,64]{1,0:T(8,128)S(1)}) custom-call(bf16[1024,1024]{1,0:T(8,128)(2,1)} %act_hbm.1, bf16[1024,256]{1,0:T(8,128)(2,1)} %grad_hbm.1, f32[64,256]{1,0:T(8,128)} %q_hbm.1, f32[1,1024,256]{2,1,0:T(8,128)} %err_hbm.1), custom_call_target="tpu_custom_call" | custom-call | tf_op jit(solution)/shard_map/powersgd/pallas_call | solution.py:324
  48.6 1.7 %residual.1 = (f32[64,256]{1,0:T(8,128)}, f32[1,1024,256]{2,1,0:T(8,128)}) custom-call(f32[1024,256]{1,0:T(8,128)S(1)} %get-tuple-element.6.merged, bf16[1024,256]{1,0:T(8,128)(2,1)S(1)} %get-tuple-element.7.basis, f32[4,32,128]{2,1,0:T(8,128)S(1)} %get-tuple-element.8.n_all, f32[64,64]{1,0:T(8,128)S(1)} %get-tuple-element.9.inverse), custom_call_target="tpu_custom_call" | custom-call | tf_op jit(solution)/shard_map/residual/pallas_call | solution.py:371

commit v9 on v8

--- a/solution.py
+++ b/solution.py
@@ -99,7 +99,7 @@
             pltpu.make_async_copy(err_hbm.at[0, at, :], err.at[at, :], load_sem.at[3 + 2 * k]),
         ])
     barrier = pltpu.get_barrier_semaphore()
-    near = [dz for dz in ring if min(dz, nz - dz) <= nz // 4]
+    near = [dz for dz in ring if min(dz, nz - dz) <= 2]
     greeted = [
         (min(dx, nx - dx) + min(dy, ny - dy), device(z, c, around(x, dx, nx), around(y, dy, ny)))
         for dx, dy in plane
@@ -144,10 +144,18 @@
             send(part.at[rows_at, span(y_at * pcols, pcols)], xy_in.at[2 * k + slot],
                  xy_send, xy_recv, device(z, c_at, x_at, y_at))
     send(part.at[span((1 - c) * half_rank, half_rank), :], from_core, core_send, core_recv, sibling)
-    for dz in (nz // 4, nz - nz // 4):
-        pl.semaphore_signal(
-            known, inc=1, device_id=device(around(z, dz, nz), c, x, y), device_id_type=MESH
-        )
+    reach = 2
+
+    def pass_on(stage):
+        if stage > 0:
+            pl.semaphore_wait(known.at[stage - 1], 2)
+        for dz in (reach, nz - reach):
+            pl.semaphore_signal(
+                known.at[stage], inc=1, device_id=device(around(z, dz, nz), c, x, y),
+                device_id_type=MESH,
+            )
+
+    pass_on(0)
     await_bytes(from_core, core_recv)
     half[...] = part[own_ranks, :] + from_core[...]
 
@@ -158,10 +166,13 @@
         x_at, y_at = around(x, dx, nx), around(y, dy, ny)
         send(piece_of(half, x_at, y_at), xy_in.at[2 * len(far) + k],
              xy_send, xy_recv, device(z, c, x_at, y_at))
+    pass_on(1)
     arriving = nt - 1 + len(far)
     xy_in[arriving] = piece_of(half, x, y)[...]
 
-    lax.fori_loop(0, 4, gradient, 0)
+    lax.fori_loop(0, 2, gradient, 0)
+    pass_on(2)
+    lax.fori_loop(2, 4, gradient, 0)
     own_rows = span(c * half_rows, half_rows)
     send(merged.at[span((1 - c) * half_rows, half_rows), :], m_core, m_send, m_recv, sibling)
 
@@ -181,7 +192,7 @@
     await_bytes(xy_in.at[pl.ds(0, arriving)], xy_recv)
     piece = jnp.sum(xy_in[...], axis=0)
     z_out[...] = piece
-    pl.semaphore_wait(known, 2)
+    pl.semaphore_wait(known.at[2], 2)
     for dz in ring:
         send(z_out, z_in.at[z], z_send, z_recv, device(around(z, dz, nz), c, x, y))
     z_in[z] = piece
@@ -362,7 +373,7 @@
             dma, dma,
             dma, dma,
             dma, dma,
-            pltpu.SemaphoreType.REGULAR,
+            pltpu.SemaphoreType.REGULAR((3,)),
         ],
         compiler_params=pltpu.CompilerParams(
             collective_id=0, has_side_effects=True, vmem_limit_bytes=20 * 1024 * 1024

time: 50.4 us -> 49.7 us (0.986)
  Pallas kernels: 49.7 us -> 49 us
    pallas_call x1, Pallas kernels: 47.9 us -> 47.2 us  [on_device(): pl.pallas_call(functools.partial(kernel, nx, ny, nz), name='powersgd', ou...]
where the time goes in v9:
time: 49.7 us; the launch traced here: 49.6 us
  Pallas kernels  49 us (99%)
  between operations  0.64 us (1%)
    pallas_call x1, Pallas kernels, on_device(): pl.pallas_call(functools.partial(kernel, nx, ny, nz), name='powersgd', ou...  47.2 us
    pallas_call x1, Pallas kernels, on_device(): pl.pallas_call(functools.partial(finish, nz * CORES), name='residual', ou...  1.74 us

profile of v9, /device:TPU:1, one launch (start us, length us, event | category | flops | bytes accessed | tf_op | source)
XLA Modules:
  0.0 49.6 jit_solution(3218057365979039141)
XLA Ops:
  0.6 47.2 %powersgd.1 = (f32[1024,256]{1,0:T(8,128)S(1)}, bf16[1024,256]{1,0:T(8,128)(2,1)S(1)}, f32[4,32,128]{2,1,0:T(8,128)S(1)}, f32[64,64]{1,0:T(8,128)S(1)}) custom-call(bf16[1024,1024]{1,0:T(8,128)(2,1)} %act_hbm.1, bf16[1024,256]{1,0:T(8,128)(2,1)} %grad_hbm.1, f32[64,256]{1,0:T(8,128)} %q_hbm.1, f32[1,1024,256]{2,1,0:T(8,128)} %err_hbm.1), custom_call_target="tpu_custom_call" | custom-call | tf_op jit(solution)/shard_map/powersgd/pallas_call | solution.py:335
  47.9 1.7 %residual.1 = (f32[64,256]{1,0:T(8,128)}, f32[1,1024,256]{2,1,0:T(8,128)}) custom-call(f32[1024,256]{1,0:T(8,128)S(1)} %get-tuple-element.6.merged, bf16[1024,256]{1,0:T(8,128)(2,1)S(1)} %get-tuple-element.7.basis, f32[4,32,128]{2,1,0:T(8,128)S(1)} %get-tuple-element.8.n_all, f32[64,64]{1,0:T(8,128)S(1)} %get-tuple-element.9.inverse), custom_call_target="tpu_custom_call" | custom-call | tf_op jit(solution)/shard_map/residual/pallas_call | solution.py:382

commit v10 on v5

--- a/solution.py
+++ b/solution.py
@@ -99,7 +99,7 @@
             pltpu.make_async_copy(err_hbm.at[0, at, :], err.at[at, :], load_sem.at[3 + 2 * k]),
         ])
     barrier = pltpu.get_barrier_semaphore()
-    near = [dz for dz in ring if min(dz, nz - dz) <= nz // 4]
+    near = [dz for dz in ring if min(dz, nz - dz) <= 2]
     greeted = [
         (min(dx, nx - dx) + min(dy, ny - dy), device(z, c, around(x, dx, nx), around(y, dy, ny)))
         for dx, dy in plane
@@ -144,10 +144,18 @@
             send(part.at[rows_at, span(y_at * pcols, pcols)], xy_in.at[2 * k + slot],
                  xy_send, xy_recv, device(z, c_at, x_at, y_at))
     send(part.at[span((1 - c) * half_rank, half_rank), :], from_core, core_send, core_recv, sibling)
-    for dz in (nz // 4, nz - nz // 4):
-        pl.semaphore_signal(
-            known, inc=1, device_id=device(around(z, dz, nz), c, x, y), device_id_type=MESH
-        )
+    reach = 2
+
+    def pass_on(stage):
+        if stage > 0:
+            pl.semaphore_wait(known.at[stage - 1], 2)
+        for dz in (reach, nz - reach):
+            pl.semaphore_signal(
+                known.at[stage], inc=1, device_id=device(around(z, dz, nz), c, x, y),
+                device_id_type=MESH,
+            )
+
+    pass_on(0)
     await_bytes(from_core, core_recv)
     half[...] = part[own_ranks, :] + from_core[...]
 
@@ -158,10 +166,13 @@
         x_at, y_at = around(x, dx, nx), around(y, dy, ny)
         send(piece_of(half, x_at, y_at), xy_in.at[2 * len(far) + k],
              xy_send, xy_recv, device(z, c, x_at, y_at))
+    pass_on(1)
     arriving = nt - 1 + len(far)
     xy_in[arriving] = piece_of(half, x, y)[...]
 
-    lax.fori_loop(0, 4, gradient, 0)
+    lax.fori_loop(0, 2, gradient, 0)
+    pass_on(2)
+    lax.fori_loop(2, 4, gradient, 0)
     own_rows = span(c * half_rows, half_rows)
     send(merged.at[span((1 - c) * half_rows, half_rows), :], m_core, m_send, m_recv, sibling)
 
@@ -181,7 +192,7 @@
     await_bytes(xy_in.at[pl.ds(0, arriving)], xy_recv)
     piece = jnp.sum(xy_in[...], axis=0)
     z_out[...] = piece
-    pl.semaphore_wait(known, 2)
+    pl.semaphore_wait(known.at[2], 2)
     for dz in ring:
         send(z_out, z_in.at[z], z_send, z_recv, device(around(z, dz, nz), c, x, y))
     z_in[z] = piece
@@ -344,7 +355,7 @@
             dma, dma,
             dma, dma,
             dma, dma,
-            pltpu.SemaphoreType.REGULAR,
+            pltpu.SemaphoreType.REGULAR((3,)),
         ],
         compiler_params=pltpu.CompilerParams(
             collective_id=0, has_side_effects=True, vmem_limit_bytes=20 * 1024 * 1024

time: 50.3 us -> 49.7 us (0.988)
  Pallas kernels: 49.6 us -> 48.9 us
    pallas_call x1, Pallas kernels: 47.9 us -> 47.2 us  [on_device(): pl.pallas_call(functools.partial(kernel, nx, ny, nz), name='powersgd', ou...]
where the time goes in v10:
time: 49.7 us; the launch traced here: 49.5 us
  Pallas kernels  48.9 us (98%)
  between operations  0.64 us (1%)
    pallas_call x1, Pallas kernels, on_device(): pl.pallas_call(functools.partial(kernel, nx, ny, nz), name='powersgd', ou...  47.2 us
    pallas_call x1, Pallas kernels, on_device(): pl.pallas_call(functools.partial(finish, nz * CORES), name='residual', ou...  1.66 us

profile of v10, /device:TPU:1, one launch (start us, length us, event | category | flops | bytes accessed | tf_op | source)
XLA Modules:
  0.0 49.5 jit_solution(17412126502867655857)
XLA Ops:
  0.6 47.2 %powersgd.1 = (f32[1024,256]{1,0:T(8,128)S(1)}, bf16[1024,256]{1,0:T(8,128)(2,1)S(1)}, f32[4,32,128]{2,1,0:T(8,128)S(1)}, f32[64,64]{1,0:T(8,128)S(1)}) custom-call(bf16[1024,1024]{1,0:T(8,128)(2,1)} %act_hbm.1, bf16[1024,256]{1,0:T(8,128)(2,1)} %grad_hbm.1, f32[64,256]{1,0:T(8,128)} %q_hbm.1, f32[1,1024,256]{2,1,0:T(8,128)} %err_hbm.1), custom_call_target="tpu_custom_call" | custom-call | tf_op jit(solution)/shard_map/powersgd/pallas_call | solution.py:317
  47.9 1.7 %residual.1 = (f32[64,256]{1,0:T(8,128)}, f32[1,1024,256]{2,1,0:T(8,128)}) custom-call(f32[1024,256]{1,0:T(8,128)S(1)} %get-tuple-element.6.merged, bf16[1024,256]{1,0:T(8,128)(2,1)S(1)} %get-tuple-element.7.basis, f32[4,32,128]{2,1,0:T(8,128)S(1)} %get-tuple-element.8.n_all, f32[64,64]{1,0:T(8,128)S(1)} %get-tuple-element.9.inverse), custom_call_target="tpu_custom_call" | custom-call | tf_op jit(solution)/shard_map/residual/pallas_call | solution.py:364
